TPU v7x, 512 devices: a whole 4x8x8 slice. The times are simulated.
512 devices in a mesh: gx: 16 (over y, z_hi), gy: 32 (over z_lo, x, core).
Axes of the slice: x: 4, y: 8, z: 8 (z_hi: 2, z_lo: 4; z = z_hi * 4 + z_lo), core: 2. Of those that a mesh axis runs over, the one named last changes fastest.
Arguments:
- tokens: bfloat16 [2, 192, 12288], P(None, None, 'gx'), may hold values from -6 to 6
- gate_weight: bfloat16 [26624, 12288], P('gy', 'gx'), may hold values from -0.0546875 to 0.0546875
- up_weight: bfloat16 [26624, 12288], P('gy', 'gx'), may hold values from -0.0546875 to 0.0546875
- down_weight: bfloat16 [26624, 12288], P('gy', 'gx'), may hold values from -0.0390625 to 0.0390625
Outputs:
- mixed_out: bfloat16 [2, 192, 12288], P(None, None, 'gx')
All inputs are finite; a program needn't handle non-finite values.
Results may differ from a plain program's by a relative error of at most 0.0051.
Values may be sent and summed in bfloat16 or wider, within the bound.
No kernel may reach another device: no remote copies, remote signals or barrier semaphores. Data moves between devices by JAX's collectives and lax.ppermute only.
A program may use at most 64 MiB of HBM per device.

v0:
```python
import jax
import jax.numpy as jnp
from jax import lax
from jax.sharding import PartitionSpec as P


def project(row_piece, weight):
    return lax.dot_general(
        row_piece, weight, (((1,), (1,)), ((), ())), preferred_element_type=jnp.float32
    )


def apply_layer(tok_rows, gate_weight, up_weight, down_weight):
    local_ff = gate_weight.shape[0]
    row_piece = tok_rows
    summed = lax.psum_scatter(
        jnp.concatenate((project(row_piece, gate_weight), project(row_piece, up_weight)), axis=1),
        "gx",
        scatter_dimension=0,
        tiled=True,
    )
    hidden_share = (jax.nn.silu(summed[:, :local_ff]) * summed[:, local_ff:]).astype(jnp.bfloat16)
    hidden = lax.all_gather(hidden_share, "gx", axis=0, tiled=True)
    row_piece = hidden
    out_share = lax.psum_scatter(
        jnp.dot(row_piece, down_weight, preferred_element_type=jnp.float32),
        "gy",
        scatter_dimension=0,
        tiled=True,
    ).astype(jnp.bfloat16)
    return lax.all_gather(out_share, "gy", axis=0, tiled=True)


def body(tokens, gate_weight, up_weight, down_weight):
    step_count, batch_rows, feat_width = tokens.shape
    blocks = [tokens.reshape(step_count * batch_rows, feat_width)]
    results = [
        apply_layer(block_rows, gate_weight, up_weight, down_weight) for block_rows in blocks
    ]
    return results[0].reshape(step_count, batch_rows, feat_width)


def solution(mesh):
    in_specs = (P(None, None, "gx"), P("gy", "gx"), P("gy", "gx"), P("gy", "gx"))
    out_specs = P(None, None, "gx")
    return jax.shard_map(body, mesh=mesh, in_specs=in_specs, out_specs=out_specs, check_vma=False)
```

profile of v0, /device:TPU:1, one launch (start us, length us, event | category | flops | bytes accessed | tf_op | source)
XLA Modules:
  0.0 534.5 jit_solution(13085924167219473024)
XLA Ops:
  6.5 0.0 copy-start
  6.5 0.0 all-reduce.5.cloned.1.call-start
  6.5 1.3 copy-done
  7.8 0.0 copy-start.1
  7.8 0.0 copy-start.2
  7.8 2.0 fusion.3
  9.9 0.0 copy-done.1
  9.9 0.0 copy-done.2
  9.9 0.8 fusion.4
  10.8 1.7 pad_maximum_fusion
  12.4 0.0 all-reduce.5.cloned.1.call-update
  12.5 1.3 dynamic-slice
  14.4 296.8 %all-reduce.5.cloned.1.call-done = f32[384,1664]{0,1:T(8,128)} async-done(((f32[384,1664]{0,1:T(8,128)}), f32[384,1664]{0,1:T(8,128)}) %all-reduce.5.cloned.1.call-update) | async-done | bytes 2555920
  311.2 1.7 constant_dynamic-slice_fusion
  312.9 0.2 copy.10
  313.0 0.2 copy.11
  313.2 0.1 multiply_convert_fusion
  313.3 54.7 %all_gather.6 = bf16[384,832]{1,0:T(8,128)(2,1)S(1)} all-gather(bf16[24,832]{1,0:T(8,128)(2,1)S(1)} %multiply_convert_fusion), channel_id=1, replica_groups=mesh['gx'=16,'gy'=32] {'gx'}, dimensions={0}, use_global_device_ids=true | all-gather | bytes 678912 | tf_op jit(solution)/shard_map/all_gather | solution.py:23
  368.0 2.1 fusion.5
  370.1 91.3 %fusion = f32[16,768]{1,0:T(8,128)S(1)} fusion(f32[384,768]{1,0:T(8,128)S(1)} %fusion.5), kind=kCustom, calls=%all-reduce-scatter | all-reduce-scatter fusion | flops 393217 | bytes 1230848
  461.4 1.9 collective-permute-start
  463.3 1.3 collective-permute-start.1
  464.6 1.3 collective-permute-start.7
  465.9 1.3 collective-permute-start.2
  467.2 1.3 collective-permute-start.3
  468.5 0.0 collective-permute-done.7
  468.5 1.3 collective-permute-start.4
  469.8 0.0 collective-permute-done
  469.8 9.1 %collective-permute-start.5 = (bf16[16,768]{1,0:T(8,128)(2,1)S(1)}, bf16[16,768]{1,0:T(8,128)(2,1)S(1)}, u32[]{:S(2)}, u32[]{:S(2)}) collective-permute-start(bf16[16,768]{1,0:T(8,128)(2,1)S(1)} %convert.15), channel_id=1, source_target_pairs={{0,6},{1,7},{2,8},{3,9},{4,10},{5,11},{6,12},{7,13},{8,14},{9,15},... | collective-permute-start | bytes 73736
  478.9 0.0 collective-permute-done.1
  478.9 3.9 collective-permute-start.6
  482.8 1.3 dynamic-slice.8
  484.7 0.0 collective-permute-done.2
  484.7 0.0 collective-permute-done.3
  484.7 0.0 collective-permute-done.4
  484.8 0.0 collective-permute-done.5
  484.8 0.0 collective-permute-done.6
  484.8 1.1 concatenate.4
  486.0 40.7 %all-gather = bf16[32,12,768]{2,1,0:T(8,128)(2,1)S(1)} all-gather(bf16[1,12,768]{2,1,0:T(8,128)(2,1)S(1)} %fusion.1), channel_id=1, replica_groups=mesh['gx'=16,'gy'=32] {'gy'}, dimensions={0}, use_global_device_ids=true | all-gather | bytes 608256 | tf_op jit(solution)/shard_map/all_gather | solution.py:31
  526.7 0.9 reshape.7
  (3 shorter events, 0.0 us)
Async XLA Ops:
  6.5 1.3 copy-start
  6.5 304.6 %all-reduce.5.cloned.1.call-start = ((), (), s32[]{:S(2)}) async-start(), calls=%async_computation | async-start | bytes 5111808
  7.8 2.0 copy-start.1
  7.8 2.1 copy-start.2
  461.4 8.5 %collective-permute-start = (bf16[16,768]{1,0:T(8,128)(2,1)S(1)}, bf16[16,768]{1,0:T(8,128)(2,1)S(1)}, u32[]{:S(2)}, u32[]{:S(2)}) collective-permute-start(bf16[16,768]{1,0:T(8,128)(2,1)S(1)} %convert.15), channel_id=1, source_target_pairs={{0,1},{1,2},{2,3},{3,4},{4,5},{5,6},{6,7},{7,8},{8,9},{9,10},{10,1... | collective-permute-start | bytes 73736
  463.3 15.6 %collective-permute-start.1 = (bf16[16,768]{1,0:T(8,128)(2,1)S(1)}, bf16[16,768]{1,0:T(8,128)(2,1)S(1)}, u32[]{:S(2)}, u32[]{:S(2)}) collective-permute-start(bf16[16,768]{1,0:T(8,128)(2,1)S(1)} %convert.15), channel_id=1, source_target_pairs={{0,2},{1,3},{2,4},{3,5},{4,6},{5,7},{6,8},{7,9},{8,10},{9,11},{10,... | collective-permute-start | bytes 73736
  464.6 3.9 collective-permute-start.7
  465.9 18.8 %collective-permute-start.2 = (bf16[16,768]{1,0:T(8,128)(2,1)S(1)}, bf16[16,768]{1,0:T(8,128)(2,1)S(1)}, u32[]{:S(2)}, u32[]{:S(2)}) collective-permute-start(bf16[16,768]{1,0:T(8,128)(2,1)S(1)} %convert.15), channel_id=1, source_target_pairs={{0,3},{1,4},{2,5},{3,6},{4,7},{5,8},{6,9},{7,10},{8,11},{9,12},{10... | collective-permute-start | bytes 73736
  467.2 17.5 %collective-permute-start.3 = (bf16[16,768]{1,0:T(8,128)(2,1)S(1)}, bf16[16,768]{1,0:T(8,128)(2,1)S(1)}, u32[]{:S(2)}, u32[]{:S(2)}) collective-permute-start(bf16[16,768]{1,0:T(8,128)(2,1)S(1)} %convert.15), channel_id=1, source_target_pairs={{0,4},{1,5},{2,6},{3,7},{4,8},{5,9},{6,10},{7,11},{8,12},{9,13},{1... | collective-permute-start | bytes 73736
  468.5 16.2 %collective-permute-start.4 = (bf16[16,768]{1,0:T(8,128)(2,1)S(1)}, bf16[16,768]{1,0:T(8,128)(2,1)S(1)}, u32[]{:S(2)}, u32[]{:S(2)}) collective-permute-start(bf16[16,768]{1,0:T(8,128)(2,1)S(1)} %convert.15), channel_id=1, source_target_pairs={{0,5},{1,6},{2,7},{3,8},{4,9},{5,10},{6,11},{7,12},{8,13},{9,14},{... | collective-permute-start | bytes 73736
  469.8 14.9 %collective-permute-start.5 = (bf16[16,768]{1,0:T(8,128)(2,1)S(1)}, bf16[16,768]{1,0:T(8,128)(2,1)S(1)}, u32[]{:S(2)}, u32[]{:S(2)}) collective-permute-start(bf16[16,768]{1,0:T(8,128)(2,1)S(1)} %convert.15), channel_id=1, source_target_pairs={{0,6},{1,7},{2,8},{3,9},{4,10},{5,11},{6,12},{7,13},{8,14},{9,15},... | collective-permute-start | bytes 73736
  478.9 5.9 %collective-permute-start.6 = (bf16[16,768]{1,0:T(8,128)(2,1)S(1)}, bf16[16,768]{1,0:T(8,128)(2,1)S(1)}, u32[]{:S(2)}, u32[]{:S(2)}) collective-permute-start(bf16[16,768]{1,0:T(8,128)(2,1)S(1)} %convert.15), channel_id=1, source_target_pairs={{0,7},{1,8},{2,9},{3,10},{4,11},{5,12},{6,13},{7,14},{8,15},{9,16}... | collective-permute-start | bytes 73736
Sparse Core Ops, SparseCore 0:
  12.6 298.5 all-reduce.4
where the time goes:
time: 538 us; the launch traced here: 534 us
  waiting for transfers between devices  297 us (55%)
  blocking collectives  187 us (35%)
  starting transfers between devices  21.3 us (4%)
  between operations  14.9 us (3%)
  local copies, waits for them, and re-layouts  8 us (1%)
    unnamed x10, waiting for transfers between devices  297 us
    unnamed x1, blocking collectives  91.3 us
    all_gather x1, blocking collectives, apply_layer(): hidden = lax.all_gather(hidden_share, 'gx', axis=0, tiled=True)  54.7 us
    all_gather x1, blocking collectives, apply_layer(): return lax.all_gather(out_share, 'gy', axis=0, tiled=True)  40.7 us
    unnamed x9, starting transfers between devices  21.3 us
  transfers between devices with their start and end apart: 9, of which 1 were waited for; matrix products, arithmetic and copies ran while one was open for 0% of the time, Pallas kernels for 0%

commit v1 on v0

v1 whole, which is shorter than its diff:
```python
import jax
import jax.numpy as jnp
from jax import lax
from jax.sharding import Mesh, PartitionSpec as P

GX = ("y", "zh")
PLANE = ("zl", "x")


def project(rows, weight):
    return lax.dot_general(rows, weight, (((1,), (1,)), ((), ())), preferred_element_type=jnp.float32)


def exchange(blocks, axes):
    return lax.all_to_all(blocks, axes, 0, 0, tiled=True)


def total(blocks):
    return jnp.sum(blocks.astype(jnp.float32), axis=0)


def spread(block, axes, count):
    return exchange(jnp.broadcast_to(block[None], (count, *block.shape)), axes)


def body(tokens, gate_weight, up_weight, down_weight):
    steps, batch, width = tokens.shape
    rows = steps * batch
    local_ff = gate_weight.shape[0]
    flat = tokens.reshape(rows, width)
    partial_sums = jnp.concatenate((project(flat, gate_weight), project(flat, up_weight)), axis=1)
    sent = partial_sums.astype(jnp.bfloat16).reshape(16, rows // 16, 2 * local_ff)
    summed = total(exchange(sent, GX))
    share = (jax.nn.silu(summed[:, :local_ff]) * summed[:, local_ff:]).astype(jnp.bfloat16)
    hidden = spread(share, GX, 16).reshape(rows, local_ff)
    partial_out = jnp.dot(hidden, down_weight, preferred_element_type=jnp.float32).astype(jnp.bfloat16)
    half = width // 2
    pair = exchange(jnp.stack((partial_out[:, :half], partial_out[:, half:])), "c")
    chip_sum = total(pair).astype(jnp.bfloat16).reshape(16, rows // 16, half)
    out_share = total(exchange(chip_sum, PLANE)).astype(jnp.bfloat16)
    out_half = spread(out_share, PLANE, 16).reshape(rows, half)
    out = lax.all_gather(out_half, "c", axis=1, tiled=True)
    return out.reshape(steps, batch, width)


def solution(mesh):
    fine = Mesh(mesh.devices.reshape(8, 2, 4, 4, 2), ("y", "zh", "zl", "x", "c"))
    gy = ("zl", "x", "c")
    in_specs = (P(None, None, GX), P(gy, GX), P(gy, GX), P(gy, GX))
    return jax.shard_map(body, mesh=fine, in_specs=in_specs, out_specs=P(None, None, GX), check_vma=False)
```

time: 538 us -> 130 us (0.24)
  waiting for transfers between devices: 297 us -> 0 us
  blocking collectives: 187 us -> 123 us
  starting transfers between devices: 21.3 us -> 0 us
  between operations: 14.9 us -> 0.1 us
  local copies, waits for them, and re-layouts: 8 us -> 2.27 us
    unnamed x10 -> x0, waiting for transfers between devices: 297 us -> none
    all_to_all x0 -> x5, blocking collectives: none -> 119 us  [exchange(): return lax.all_to_all(blocks, axes, 0, 0, tiled=True)]
    unnamed x1 -> x0, blocking collectives: 91.3 us -> none
    all_gather x2 -> x1, blocking collectives: 95.5 us -> 4.26 us  [body(): out = lax.all_gather(out_half, 'c', axis=1, tiled=True)]
    unnamed x9 -> x0, starting transfers between devices: 21.3 us -> none
  transfers between devices with their start and end apart: 9 -> 0, of which waited for: 1 -> 0; matrix products, arithmetic and copies ran while one was open for 0% -> 0% of each run, Pallas kernels for 0% -> 0%
where the time goes in v1:
time: 130 us
  blocking collectives  123 us (95%)
  matrix products  3.6 us (3%)
  local copies, waits for them, and re-layouts  2.27 us (2%)
    all_to_all x5, blocking collectives, exchange(): return lax.all_to_all(blocks, axes, 0, 0, tiled=True)  119 us
    all_gather x1, blocking collectives, body(): out = lax.all_gather(out_half, 'c', axis=1, tiled=True)  4.26 us
    dot_general x2, matrix products, project(): lax.dot_general(rows, weight, (((1,), (1,)), ((), ())), preferred_element...  2.82 us

profile of v1, /device:TPU:1, one launch (start us, length us, event | category | flops | bytes accessed | tf_op | source)
XLA Modules:
  0.0 129.7 jit_solution(956132729581297244)
XLA Ops:
  0.0 0.0 copy-start
  0.0 1.3 %copy-done = bf16[832,768]{1,0:T(8,128)(2,1)S(1)} copy-done((bf16[832,768]{1,0:T(8,128)(2,1)S(1)}, bf16[832,768]{1,0:T(8,128)(2,1)}, u32[]{:S(2)}) %copy-start) | copy-done | bytes 1277976
  1.3 0.0 copy-start.1
  1.3 0.0 copy-start.3
  1.3 2.0 %convolution_convert_fusion = bf16[16,24,832]{2,1,0:T(8,128)(2,1)S(1)} fusion(bf16[16,24,768]{2,1,0:T(8,128)(2,1)} %bitcast.23, bf16[832,768]{1,0:T(8,128)(2,1)S(1)} %copy-done), kind=kOutput, calls=%fused_computation.1 | convolution fusion | flops 491053056 | bytes 2506752 | tf_op jit(solution)/shard_map/dot_general | solution.py:11
  3.3 0.0 copy-done.1
  3.3 0.0 copy-done.3
  3.3 0.8 convolution_convert_fusion.1
  4.2 0.3 pad_maximum_fusion
  4.5 53.1 %all_to_all.25 = bf16[16,24,1664]{2,1,0:T(8,128)(2,1)S(1)} all-to-all(bf16[16,24,1664]{2,1,0:T(8,128)(2,1)S(1)} %pad_maximum_fusion), channel_id=1, replica_groups=mesh['y'=8,'zh'=2,'zl'=4,'x'=4,'c'=2] {'y','zh'}, dimensions={0} | all-to-all | bytes 2555904 | tf_op jit(solution)/shard_map/all_to_all | solution.py:15
  57.6 0.2 convert_reduce_fusion
  57.8 0.0 copy-start.2
  57.8 0.1 fusion.2
  57.9 0.1 broadcast_in_dim.4
  58.0 30.1 %all_to_all.26 = bf16[16,24,832]{2,1,0:T(8,128)(2,1)S(1)} all-to-all(bf16[16,24,832]{2,1,0:T(8,128)(2,1)S(1)} %broadcast_in_dim.4), channel_id=1, replica_groups=mesh['y'=8,'zh'=2,'zl'=4,'x'=4,'c'=2] {'y','zh'}, dimensions={0} | all-to-all | bytes 1277952 | tf_op jit(solution)/shard_map/all_to_all | solution.py:15
  88.1 0.0 copy-done.2
  88.1 0.8 convolution_convert_fusion.2
  88.9 0.1 slice_bitcast_fusion.1
  88.9 0.1 pad_maximum_fusion.1
  89.0 5.4 %all_to_all.27 = bf16[2,384,384]{2,1,0:T(8,128)(2,1)S(1)} all-to-all(bf16[2,384,384]{2,1,0:T(8,128)(2,1)S(1)} %pad_maximum_fusion.1), channel_id=1, replica_groups=mesh['y'=8,'zh'=2,'zl'=4,'x'=4,'c'=2] {'c'}, dimensions={0} | all-to-all | bytes 1179648 | tf_op jit(solution)/shard_map/all_to_all | solution.py:15
  94.4 0.2 reduce_sum.34
  94.6 15.9 %all_to_all.28 = bf16[16,24,384]{2,1,0:T(8,128)(2,1)S(1)} all-to-all(bf16[16,24,384]{2,1,0:T(8,128)(2,1)S(1)} %bitcast.20), channel_id=1, replica_groups=mesh['y'=8,'zh'=2,'zl'=4,'x'=4,'c'=2] {'zl','x'}, dimensions={0} | all-to-all | bytes 589824 | tf_op jit(solution)/shard_map/all_to_all | solution.py:15
  110.6 14.0 %all_to_all.29 = bf16[16,24,384]{2,1,0:T(8,128)(2,1)S(1)} all-to-all(bf16[16,24,384]{2,1,0:T(8,128)(2,1)S(1)} %broadcast_in_dim.5), channel_id=1, replica_groups=mesh['y'=8,'zh'=2,'zl'=4,'x'=4,'c'=2] {'zl','x'}, dimensions={0} | all-to-all | bytes 589824 | tf_op jit(solution)/shard_map/all_to_all | solution.py:15
  124.6 4.3 %all_gather.3 = bf16[384,768]{1,0:T(8,128)(2,1)S(1)} all-gather(bf16[384,384]{1,0:T(8,128)(2,1)S(1)} %bitcast.21), channel_id=1, replica_groups=mesh['y'=8,'zh'=2,'zl'=4,'x'=4,'c'=2] {'c'}, dimensions={1}, use_global_device_ids=true | all-gather | bytes 884736 | tf_op jit(solution)/shard_map/all_gather | solution.py:42
  128.9 0.8 copy.6
  (2 shorter events, 0.1 us)
Async XLA Ops:
  0.0 1.3 %copy-start = (bf16[832,768]{1,0:T(8,128)(2,1)S(1)}, bf16[832,768]{1,0:T(8,128)(2,1)}, u32[]{:S(2)}) copy-start(bf16[832,768]{1,0:T(8,128)(2,1)} %param.6) | copy-start | bytes 3833860
  1.3 2.0 %copy-start.1 = (bf16[832,768]{1,0:T(8,128)(2,1)S(1)}, bf16[832,768]{1,0:T(8,128)(2,1)}, u32[]{:S(2)}) copy-start(bf16[832,768]{1,0:T(8,128)(2,1)} %param.5) | copy-start | bytes 3833860
  1.3 2.0 %copy-start.3 = (bf16[2,192,768]{2,1,0:T(8,128)(2,1)S(1)}, bf16[2,192,768]{2,1,0:T(8,128)(2,1)}, u32[]{:S(2)}) copy-start(bf16[2,192,768]{2,1,0:T(8,128)(2,1)} %param.4) | copy-start | bytes 1769476
  57.8 30.3 %copy-start.2 = (bf16[832,768]{1,0:T(8,128)(2,1)S(1)}, bf16[832,768]{1,0:T(8,128)(2,1)}, u32[]{:S(2)}) copy-start(bf16[832,768]{1,0:T(8,128)(2,1)} %param.7) | copy-start | bytes 3833860

commit v2 on v1

v2 whole, which is shorter than its diff:
```python
import jax
import jax.numpy as jnp
from jax import lax
from jax.sharding import Mesh, PartitionSpec as P

PLANE = ("zl", "x")
SPLIT = 448


def project(rows, weight):
    return lax.dot_general(rows, weight, (((1,), (1,)), ((), ())), preferred_element_type=jnp.float32)


def pair(rows, gate_weight, up_weight):
    return jnp.concatenate((project(rows, gate_weight), project(rows, up_weight)), axis=1)


def exchange(blocks, axes):
    return lax.all_to_all(blocks, axes, 0, 0, tiled=True)


def spread(block, axes, count):
    return exchange(jnp.broadcast_to(block[None], (count, *block.shape)), axes)


def swap(block):
    return lax.ppermute(block, "zh", [(0, 1), (1, 0)])


def total(blocks):
    return jnp.sum(blocks.astype(jnp.float32), axis=0)


def activate(sums):
    units = sums.shape[-1] // 2
    return (jax.nn.silu(sums[..., :units]) * sums[..., units:]).astype(jnp.bfloat16)


def body(tokens, gate_weight, up_weight, down_weight):
    steps, batch, width = tokens.shape
    rows = steps * batch
    flat = tokens.reshape(rows, width)
    low = lax.axis_index("zh") == 0

    def mine(blocks):
        return jnp.where(low, blocks[0], blocks[1])

    def other(blocks):
        return jnp.where(low, blocks[1], blocks[0])

    def both(own, far):
        return jnp.where(low, jnp.stack((own, far)), jnp.stack((far, own)))

    q = pair(flat, gate_weight[SPLIT:], up_weight[SPLIT:]).reshape(2, rows // 2, -1)
    q_far = swap(other(q).astype(jnp.bfloat16))
    p = pair(flat, gate_weight[:SPLIT], up_weight[:SPLIT]).astype(jnp.bfloat16)
    p_blocks = exchange(p.reshape(8, rows // 8, -1), "y")
    q_half = (mine(q) + q_far.astype(jnp.float32)).astype(jnp.bfloat16)
    q_blocks = exchange(q_half.reshape(8, rows // 16, -1), "y")
    p_sum = total(p_blocks).reshape(2, rows // 16, -1)
    p_far = swap(other(p_sum).astype(jnp.bfloat16))
    q_hidden = activate(total(q_blocks))
    p_hidden = activate(mine(p_sum) + p_far.astype(jnp.float32))

    q_half = spread(q_hidden, "y", 8).reshape(rows // 2, -1)
    p_pair = both(p_hidden, swap(p_hidden)).reshape(rows // 8, -1)
    p_all = spread(p_pair, "y", 8).reshape(rows, -1)
    q_all = both(q_half, swap(q_half)).reshape(rows, -1)
    partial_out = jnp.dot(q_all, down_weight[SPLIT:], preferred_element_type=jnp.float32) + jnp.dot(
        p_all, down_weight[:SPLIT], preferred_element_type=jnp.float32
    )

    half = width // 2
    chip = total(exchange(jnp.stack((partial_out[:, :half], partial_out[:, half:])), "c"))
    chip = chip.astype(jnp.bfloat16).reshape(16, rows // 16, half)
    out_share = total(exchange(chip, PLANE)).astype(jnp.bfloat16)
    out_half = spread(out_share, PLANE, 16).reshape(rows, half)
    out = lax.all_gather(out_half, "c", axis=1, tiled=True)
    return out.reshape(steps, batch, width)


def solution(mesh):
    fine = Mesh(mesh.devices.reshape(8, 2, 4, 4, 2), ("y", "zh", "zl", "x", "c"))
    gx, gy = ("y", "zh"), ("zl", "x", "c")
    in_specs = (P(None, None, gx), P(gy, gx), P(gy, gx), P(gy, gx))
    return jax.shard_map(body, mesh=fine, in_specs=in_specs, out_specs=P(None, None, gx), check_vma=False)
```

time: 130 us -> 162 us (1.25)
  blocking collectives: 123 us -> 61.4 us
  waiting for transfers between devices: 0 us -> 44.7 us
  starting transfers between devices: 0 us -> 44.3 us
  local copies, waits for them, and re-layouts: 2.27 us -> 4.32 us
    all_to_all x5 -> x3, blocking collectives: 119 us -> 57.1 us  [exchange(): return lax.all_to_all(blocks, axes, 0, 0, tiled=True)]
    all_to_all x0 -> x4, waiting for transfers between devices: none -> 27.9 us  [exchange(): return lax.all_to_all(blocks, axes, 0, 0, tiled=True)]
    ppermute x0 -> x4, starting transfers between devices: none -> 25.4 us  [swap(): return lax.ppermute(block, 'zh', [(0, 1), (1, 0)])]
    all_to_all x0 -> x4, starting transfers between devices: none -> 18.9 us  [exchange(): return lax.all_to_all(blocks, axes, 0, 0, tiled=True)]
    ppermute x0 -> x4, waiting for transfers between devices: none -> 16.8 us  [swap(): return lax.ppermute(block, 'zh', [(0, 1), (1, 0)])]
  transfers between devices with their start and end apart: 0 -> 8, of which waited for: 0 -> 7; matrix products, arithmetic and copies ran while one was open for 0% -> 2% of each run, Pallas kernels for 0% -> 0%
where the time goes in v2:
time: 162 us; the launch traced here: 161 us
  blocking collectives  61.4 us (38%)
  waiting for transfers between devices  44.7 us (28%)
  starting transfers between devices  44.3 us (27%)
  local copies, waits for them, and re-layouts  4.32 us (3%)
  matrix products  3.95 us (2%)
  other arithmetic  2.15 us (1%)
    all_to_all x3, blocking collectives, exchange(): return lax.all_to_all(blocks, axes, 0, 0, tiled=True)  57.1 us
    all_to_all x4, waiting for transfers between devices, exchange(): return lax.all_to_all(blocks, axes, 0, 0, tiled=True)  27.9 us
    ppermute x4, starting transfers between devices, swap(): return lax.ppermute(block, 'zh', [(0, 1), (1, 0)])  25.4 us
    all_to_all x4, starting transfers between devices, exchange(): return lax.all_to_all(blocks, axes, 0, 0, tiled=True)  18.9 us
    ppermute x4, waiting for transfers between devices, swap(): return lax.ppermute(block, 'zh', [(0, 1), (1, 0)])  16.8 us
    all_gather x1, blocking collectives, body(): out = lax.all_gather(out_half, 'c', axis=1, tiled=True)  4.26 us
  transfers between devices with their start and end apart: 8, of which 7 were waited for; matrix products, arithmetic and copies ran while one was open for 2% of the time, Pallas kernels for 0%

profile of v2, /device:TPU:1, one launch (start us, length us, event | category | flops | bytes accessed | tf_op | source)
XLA Modules:
  0.0 161.0 jit_solution(4888821899512814047)
XLA Ops:
  0.0 0.0 copy-start
  0.0 0.0 copy-start.2
  0.0 1.1 copy-done
  1.1 1.5 fusion.10
  2.6 0.0 copy-done.2
  2.6 0.5 fusion.8
  3.1 0.2 select_convert_fusion
  3.3 11.5 %collective-permute-start = (bf16[192,768]{0,1:T(8,128)(2,1)S(1)}, bf16[192,768]{0,1:T(8,128)(2,1)S(1)}, u32[]{:S(2)}, u32[]{:S(2)}) collective-permute-start(bf16[192,768]{0,1:T(8,128)(2,1)S(1)} %select_convert_fusion), channel_id=1, source_target_pairs={{0,32},{32,0},{1,33},{33,1},{2,34},{34,2},{3,35},{35,3},{4,36},{36... | collective-permute-start | bytes 884744 | tf_op jit(solution)/shard_map/ppermute | solution.py:27
  14.8 8.0 %collective-permute-done = bf16[192,768]{0,1:T(8,128)(2,1)S(1)} collective-permute-done((bf16[192,768]{0,1:T(8,128)(2,1)S(1)}, bf16[192,768]{0,1:T(8,128)(2,1)S(1)}, u32[]{:S(2)}, u32[]{:S(2)}) %collective-permute-start) | collective-permute-done | bytes 294944 | tf_op jit(solution)/shard_map/ppermute | solution.py:27
  22.8 0.3 add_convert_fusion
  23.0 0.9 copy.6
  23.9 0.0 copy-start.3
  23.9 7.9 %all-to-all-start = ((bf16[8,24,768]{2,1,0:T(8,128)(2,1)}), bf16[8,24,768]{2,1,0:T(8,128)(2,1)S(1)}, u32[]{:S(2)}, u32[]{:S(2)}) async-start(bf16[8,24,768]{2,1,0:T(8,128)(2,1)} %bitcast.1), calls=%async_computation | async-start | bytes 589824 | tf_op jit(solution)/shard_map/all_to_all | solution.py:19
  31.8 0.5 convolution_convert_fusion
  32.3 0.0 copy-done.3
  32.3 0.5 convolution_convert_fusion.1
  32.8 1.1 pad_maximum_fusion.2
  33.9 8.5 %all-to-all-done = bf16[8,24,768]{2,1,0:T(8,128)(2,1)S(1)} async-done(((bf16[8,24,768]{2,1,0:T(8,128)(2,1)}), bf16[8,24,768]{2,1,0:T(8,128)(2,1)S(1)}, u32[]{:S(2)}, u32[]{:S(2)}) %all-to-all-start) | async-done | bytes 294944 | tf_op jit(solution)/shard_map/all_to_all | solution.py:19
  42.4 3.5 %all-to-all-start.2 = ((bf16[8,48,896]{2,1,0:T(8,128)(2,1)}), bf16[8,48,896]{2,1,0:T(8,128)(2,1)S(1)}, u32[]{:S(2)}, u32[]{:S(2)}) async-start(bf16[8,48,896]{2,1,0:T(8,128)(2,1)} %pad_maximum_fusion.2), calls=%async_computation.2 | async-start | bytes 1376256 | tf_op jit(solution)/shard_map/all_to_all | solution.py:19
  46.0 18.5 %all-to-all-done.2 = bf16[8,48,896]{2,1,0:T(8,128)(2,1)S(1)} async-done(((bf16[8,48,896]{2,1,0:T(8,128)(2,1)}), bf16[8,48,896]{2,1,0:T(8,128)(2,1)S(1)}, u32[]{:S(2)}, u32[]{:S(2)}) %all-to-all-start.2) | async-done | bytes 688160 | tf_op jit(solution)/shard_map/all_to_all | solution.py:19
  64.6 0.1 convert_reduce_fusion
  64.7 1.9 %collective-permute-start.2 = (bf16[24,896]{1,0:T(8,128)(2,1)S(1)}, bf16[24,896]{1,0:T(8,128)(2,1)S(1)}, u32[]{:S(2)}, u32[]{:S(2)}) collective-permute-start(bf16[24,896]{1,0:T(8,128)(2,1)S(1)} %select_convert_fusion.1), channel_id=1, source_target_pairs={{0,32},{32,0},{1,33},{33,1},{2,34},{34,2},{3,35},{35,3},{4,36},{36... | collective-permute-start | bytes 129032 | tf_op jit(solution)/shard_map/ppermute | solution.py:27
  66.7 0.7 broadcast_in_dim.6
  67.3 3.4 %all-to-all-start.1 = ((bf16[8,24,384]{2,1,0:T(8,128)(2,1)}), bf16[8,24,384]{2,1,0:T(8,128)(2,1)S(1)}, u32[]{:S(2)}, u32[]{:S(2)}) async-start(bf16[8,24,384]{2,1,0:T(8,128)(2,1)} %broadcast_in_dim.6), calls=%async_computation.1 | async-start | bytes 294912 | tf_op jit(solution)/shard_map/all_to_all | solution.py:19
  70.7 0.0 copy-start.1
  70.7 2.6 %collective-permute-done.2 = bf16[24,896]{1,0:T(8,128)(2,1)S(1)} collective-permute-done((bf16[24,896]{1,0:T(8,128)(2,1)S(1)}, bf16[24,896]{1,0:T(8,128)(2,1)S(1)}, u32[]{:S(2)}, u32[]{:S(2)}) %collective-permute-start.2) | collective-permute-done | bytes 43040 | tf_op jit(solution)/shard_map/ppermute | solution.py:27
  73.4 0.1 fusion.12
  73.5 4.8 %collective-permute-start.3 = (bf16[24,448]{1,0:T(8,128)(2,1)S(1)}, bf16[24,448]{1,0:T(8,128)(2,1)S(1)}, u32[]{:S(2)}, u32[]{:S(2)}) collective-permute-start(bf16[24,448]{1,0:T(8,128)(2,1)S(1)} %fusion.12), channel_id=1, source_target_pairs={{0,32},{32,0},{1,33},{33,1},{2,34},{34,2},{3,35},{35,3},{4,36},{36... | collective-permute-start | bytes 64520 | tf_op jit(solution)/shard_map/ppermute | solution.py:27
  78.2 0.1 fusion.20
  78.3 3.6 %collective-permute-done.3 = bf16[24,448]{1,0:T(8,128)(2,1)S(1)} collective-permute-done((bf16[24,448]{1,0:T(8,128)(2,1)S(1)}, bf16[24,448]{1,0:T(8,128)(2,1)S(1)}, u32[]{:S(2)}, u32[]{:S(2)}) %collective-permute-start.3) | collective-permute-done | bytes 21536 | tf_op jit(solution)/shard_map/ppermute | solution.py:27
  82.0 0.0 all-to-all-done.1
  82.0 0.8 broadcast_in_dim.7
  82.8 4.0 %all-to-all-start.3 = ((bf16[8,48,448]{2,1,0:T(8,128)(2,1)}), bf16[8,48,448]{2,1,0:T(8,128)(2,1)S(1)}, u32[]{:S(2)}, u32[]{:S(2)}) async-start(bf16[8,48,448]{2,1,0:T(8,128)(2,1)} %broadcast_in_dim.7), calls=%async_computation.3 | async-start | bytes 786432 | tf_op jit(solution)/shard_map/all_to_all | solution.py:19
  86.8 7.3 %collective-permute-start.1 = (bf16[192,384]{1,0:T(8,128)(2,1)S(1)}, bf16[192,384]{1,0:T(8,128)(2,1)S(1)}, u32[]{:S(2)}, u32[]{:S(2)}) collective-permute-start(bf16[192,384]{1,0:T(8,128)(2,1)S(1)} %bitcast.40), channel_id=1, source_target_pairs={{0,32},{32,0},{1,33},{33,1},{2,34},{34,2},{3,35},{35,3},{4,36},{36... | collective-permute-start | bytes 442376 | tf_op jit(solution)/shard_map/ppermute | solution.py:27
  94.1 2.6 %collective-permute-done.1 = bf16[192,384]{1,0:T(8,128)(2,1)S(1)} collective-permute-done((bf16[192,384]{1,0:T(8,128)(2,1)S(1)}, bf16[192,384]{1,0:T(8,128)(2,1)S(1)}, u32[]{:S(2)}, u32[]{:S(2)}) %collective-permute-start.1) | collective-permute-done | bytes 147488 | tf_op jit(solution)/shard_map/ppermute | solution.py:27
  96.7 0.1 maximum_select_fusion
  96.7 0.8 all-to-all-done.3
  97.5 0.0 copy-done.1
  97.5 0.5 fusion.3
  98.0 0.5 convolution_add_fusion
  98.5 0.1 slice_bitcast_fusion.1
  98.6 0.1 pad_maximum_fusion
  98.7 19.6 %all_to_all.35 = f32[2,384,384]{2,1,0:T(8,128)S(1)} all-to-all(f32[2,384,384]{2,1,0:T(8,128)S(1)} %pad_maximum_fusion), channel_id=1, replica_groups=mesh['y'=8,'zh'=2,'zl'=4,'x'=4,'c'=2] {'c'}, dimensions={0} | all-to-all | bytes 2359296 | tf_op jit(solution)/shard_map/all_to_all | solution.py:19
  118.3 0.1 reduce_sum.41
  118.3 23.5 %all_to_all.36 = bf16[16,24,384]{2,1,0:T(8,128)(2,1)S(1)} all-to-all(bf16[16,24,384]{2,1,0:T(8,128)(2,1)S(1)} %bitcast.39), channel_id=1, replica_groups=mesh['y'=8,'zh'=2,'zl'=4,'x'=4,'c'=2] {'zl','x'}, dimensions={0} | all-to-all | bytes 589824 | tf_op jit(solution)/shard_map/all_to_all | solution.py:19
  142.0 14.0 %all_to_all.37 = bf16[16,24,384]{2,1,0:T(8,128)(2,1)S(1)} all-to-all(bf16[16,24,384]{2,1,0:T(8,128)(2,1)S(1)} %broadcast_in_dim.8), channel_id=1, replica_groups=mesh['y'=8,'zh'=2,'zl'=4,'x'=4,'c'=2] {'zl','x'}, dimensions={0} | all-to-all | bytes 589824 | tf_op jit(solution)/shard_map/all_to_all | solution.py:19
  155.9 4.3 %all_gather.3 = bf16[384,768]{1,0:T(8,128)(2,1)S(1)} all-gather(bf16[384,384]{1,0:T(8,128)(2,1)S(1)} %bitcast.38), channel_id=1, replica_groups=mesh['y'=8,'zh'=2,'zl'=4,'x'=4,'c'=2] {'c'}, dimensions={1}, use_global_device_ids=true | all-gather | bytes 884736 | tf_op jit(solution)/shard_map/all_gather | solution.py:78
  160.2 0.8 copy.8
  (7 shorter events, 0.2 us)
Async XLA Ops:
  0.0 1.1 copy-start
  0.0 2.6 %copy-start.2 = (bf16[832,768]{1,0:T(8,128)(2,1)S(1)}, bf16[832,768]{1,0:T(8,128)(2,1)}, u32[]{:S(2)}) copy-start(bf16[832,768]{1,0:T(8,128)(2,1)} %param.6) | copy-start | bytes 3833860
  3.3 19.4 %collective-permute-start = (bf16[192,768]{0,1:T(8,128)(2,1)S(1)}, bf16[192,768]{0,1:T(8,128)(2,1)S(1)}, u32[]{:S(2)}, u32[]{:S(2)}) collective-permute-start(bf16[192,768]{0,1:T(8,128)(2,1)S(1)} %select_convert_fusion), channel_id=1, source_target_pairs={{0,32},{32,0},{1,33},{33,1},{2,34},{34,2},{3,35},{35,3},{4,36},{36... | collective-permute-start | bytes 884744 | tf_op jit(solution)/shard_map/ppermute | solution.py:27
  23.9 8.4 %copy-start.3 = (bf16[832,768]{1,0:T(8,128)(2,1)S(1)}, bf16[832,768]{1,0:T(8,128)(2,1)}, u32[]{:S(2)}) copy-start(bf16[832,768]{1,0:T(8,128)(2,1)} %param.5) | copy-start | bytes 3833860
  23.9 18.5 %all-to-all-start = ((bf16[8,24,768]{2,1,0:T(8,128)(2,1)}), bf16[8,24,768]{2,1,0:T(8,128)(2,1)S(1)}, u32[]{:S(2)}, u32[]{:S(2)}) async-start(bf16[8,24,768]{2,1,0:T(8,128)(2,1)} %bitcast.1), calls=%async_computation | async-start | bytes 589824 | tf_op jit(solution)/shard_map/all_to_all | solution.py:19
  42.4 22.1 %all-to-all-start.2 = ((bf16[8,48,896]{2,1,0:T(8,128)(2,1)}), bf16[8,48,896]{2,1,0:T(8,128)(2,1)S(1)}, u32[]{:S(2)}, u32[]{:S(2)}) async-start(bf16[8,48,896]{2,1,0:T(8,128)(2,1)} %pad_maximum_fusion.2), calls=%async_computation.2 | async-start | bytes 1376256 | tf_op jit(solution)/shard_map/all_to_all | solution.py:19
  64.7 8.7 %collective-permute-start.2 = (bf16[24,896]{1,0:T(8,128)(2,1)S(1)}, bf16[24,896]{1,0:T(8,128)(2,1)S(1)}, u32[]{:S(2)}, u32[]{:S(2)}) collective-permute-start(bf16[24,896]{1,0:T(8,128)(2,1)S(1)} %select_convert_fusion.1), channel_id=1, source_target_pairs={{0,32},{32,0},{1,33},{33,1},{2,34},{34,2},{3,35},{35,3},{4,36},{36... | collective-permute-start | bytes 129032 | tf_op jit(solution)/shard_map/ppermute | solution.py:27
  67.3 14.6 %all-to-all-start.1 = ((bf16[8,24,384]{2,1,0:T(8,128)(2,1)}), bf16[8,24,384]{2,1,0:T(8,128)(2,1)S(1)}, u32[]{:S(2)}, u32[]{:S(2)}) async-start(bf16[8,24,384]{2,1,0:T(8,128)(2,1)} %broadcast_in_dim.6), calls=%async_computation.1 | async-start | bytes 294912 | tf_op jit(solution)/shard_map/all_to_all | solution.py:19
  70.7 26.8 %copy-start.1 = (bf16[832,768]{1,0:T(8,128)(2,1)S(1)}, bf16[832,768]{1,0:T(8,128)(2,1)}, u32[]{:S(2)}) copy-start(bf16[832,768]{1,0:T(8,128)(2,1)} %param.7) | copy-start | bytes 3833860
  73.5 8.5 %collective-permute-start.3 = (bf16[24,448]{1,0:T(8,128)(2,1)S(1)}, bf16[24,448]{1,0:T(8,128)(2,1)S(1)}, u32[]{:S(2)}, u32[]{:S(2)}) collective-permute-start(bf16[24,448]{1,0:T(8,128)(2,1)S(1)} %fusion.12), channel_id=1, source_target_pairs={{0,32},{32,0},{1,33},{33,1},{2,34},{34,2},{3,35},{35,3},{4,36},{36... | collective-permute-start | bytes 64520 | tf_op jit(solution)/shard_map/ppermute | solution.py:27
  82.8 14.8 %all-to-all-start.3 = ((bf16[8,48,448]{2,1,0:T(8,128)(2,1)}), bf16[8,48,448]{2,1,0:T(8,128)(2,1)S(1)}, u32[]{:S(2)}, u32[]{:S(2)}) async-start(bf16[8,48,448]{2,1,0:T(8,128)(2,1)} %broadcast_in_dim.7), calls=%async_computation.3 | async-start | bytes 786432 | tf_op jit(solution)/shard_map/all_to_all | solution.py:19
  86.8 9.9 %collective-permute-start.1 = (bf16[192,384]{1,0:T(8,128)(2,1)S(1)}, bf16[192,384]{1,0:T(8,128)(2,1)S(1)}, u32[]{:S(2)}, u32[]{:S(2)}) collective-permute-start(bf16[192,384]{1,0:T(8,128)(2,1)S(1)} %bitcast.40), channel_id=1, source_target_pairs={{0,32},{32,0},{1,33},{33,1},{2,34},{34,2},{3,35},{35,3},{4,36},{36... | collective-permute-start | bytes 442376 | tf_op jit(solution)/shard_map/ppermute | solution.py:27

commit v3 on v1

v3 whole, which is shorter than its diff:
```python
import jax
import jax.numpy as jnp
from jax import lax
from jax.sharding import Mesh, PartitionSpec as P

PLANE = ("zl", "x")


def project(rows, weight):
    return lax.dot_general(rows, weight, (((1,), (1,)), ((), ())), preferred_element_type=jnp.float32)


def exchange(blocks, axes):
    return lax.all_to_all(blocks, axes, 0, 0, tiled=True)


def spread(block, axes, count):
    return exchange(jnp.broadcast_to(block[None], (count, *block.shape)), axes)


def total(blocks):
    return jnp.sum(blocks.astype(jnp.float32), axis=0)


def shift(block, step):
    return lax.ppermute(block, "y", [(i, (i + step) % 8) for i in range(8)])


def shift_by_core(block, step):
    pairs = []
    for i in range(8):
        pairs.append((2 * i, 2 * ((i + step) % 8)))
        pairs.append((2 * i + 1, 2 * ((i - step) % 8) + 1))
    return lax.ppermute(block, ("y", "c"), pairs)


def scatter_sum(parts):
    sent = [part.astype(jnp.bfloat16) for part in parts]
    first_core = lax.axis_index("c") == 0
    far = shift_by_core(sent[4], 2).astype(jnp.float32)
    up = shift(jnp.stack((sent[1], sent[3])), 1).astype(jnp.float32)
    down = shift(jnp.stack((sent[7], sent[5])), -1).astype(jnp.float32)
    zero = jnp.zeros((), jnp.float32)
    up_two = parts[2] + up[1] + jnp.where(first_core, far, zero)
    down_two = parts[6] + down[1] + jnp.where(first_core, zero, far)
    last_up = shift(up_two.astype(jnp.bfloat16), 2)
    last_down = shift(down_two.astype(jnp.bfloat16), -2)
    return parts[0] + up[0] + down[0] + last_up.astype(jnp.float32) + last_down.astype(jnp.float32)


def body(tokens, gate_weight, up_weight, down_weight):
    steps, batch, width = tokens.shape
    rows = steps * batch
    local_ff = gate_weight.shape[0]
    flat = tokens.reshape(rows, width)
    turned = lax.dynamic_slice_in_dim(
        jnp.concatenate((flat, flat)), lax.axis_index("y") * (rows // 8), rows, 0
    )
    partial_sums = jnp.concatenate((project(turned, gate_weight), project(turned, up_weight)), axis=1)
    y_sum = scatter_sum(partial_sums.reshape(8, rows // 8, 2 * local_ff))
    near = y_sum.astype(jnp.bfloat16)
    halves = total(lax.all_gather(near, "zh", axis=0))
    summed = halves + (y_sum - near.astype(jnp.float32))
    share = (jax.nn.silu(summed[:, :local_ff]) * summed[:, local_ff:]).astype(jnp.bfloat16)
    hidden = spread(share, "y", 8).reshape(rows, local_ff)
    partial_out = jnp.dot(hidden, down_weight, preferred_element_type=jnp.float32)

    half = width // 2
    first_core = lax.axis_index("c") == 0
    own = jnp.where(first_core, partial_out[:, :half], partial_out[:, half:])
    give = jnp.where(first_core, partial_out[:, half:], partial_out[:, :half]).astype(jnp.bfloat16)
    given = lax.all_gather(give, "c", axis=0)
    chip = own + jnp.where(first_core, given[1], given[0]).astype(jnp.float32)
    chip = chip.astype(jnp.bfloat16).reshape(16, rows // 16, half)
    out_share = total(exchange(chip, PLANE)).astype(jnp.bfloat16)
    out_half = spread(out_share, PLANE, 16).reshape(rows, half)
    out = lax.all_gather(out_half, "c", axis=1, tiled=True)
    return out.reshape(steps, batch, width)


def solution(mesh):
    fine = Mesh(mesh.devices.reshape(8, 2, 4, 4, 2), ("y", "zh", "zl", "x", "c"))
    gx, gy = ("y", "zh"), ("zl", "x", "c")
    in_specs = (P(None, None, gx), P(gy, gx), P(gy, gx), P(gy, gx))
    return jax.shard_map(body, mesh=fine, in_specs=in_specs, out_specs=P(None, None, gx), check_vma=False)
```

time: 130 us -> 119 us (0.915)
  blocking collectives: 123 us -> 79.7 us
  starting transfers between devices: 0 us -> 19.4 us
  waiting for transfers between devices: 0 us -> 8.69 us
  other arithmetic: 0.9 us -> 3.24 us
  local copies, waits for them, and re-layouts: 2.27 us -> 3.71 us
    all_to_all x5 -> x3, blocking collectives: 119 us -> 52.2 us  [exchange(): return lax.all_to_all(blocks, axes, 0, 0, tiled=True)]
    all_gather x0 -> x2, blocking collectives: none -> 23.3 us  [the longest x1 13.5 us: body(): halves = total(lax.all_gather(near, 'zh', axis=0))]
    ppermute x0 -> x5, starting transfers between devices: none -> 19.4 us  [the longest x4 15.3 us: shift(): return lax.ppermute(block, 'y', [(i, (i + step) % 8) for i in range(8)])]
    ppermute x0 -> x5, waiting for transfers between devices: none -> 8.69 us  [the longest x4 7.92 us: shift(): return lax.ppermute(block, 'y', [(i, (i + step) % 8) for i in range(8)])]
    convert_element_type x0 -> x6, other arithmetic: none -> 2.58 us  [the longest x1 1.12 us: scatter_sum(): down = shift(jnp.stack((sent[7], sent[5])), -1).astype(jnp.float32)]
    unnamed x9 -> x13, local copies, waits for them, and re-layouts: 2.13 us -> 2.91 us
  transfers between devices with their start and end apart: 0 -> 5, of which waited for: 0 -> 4; matrix products, arithmetic and copies ran while one was open for 0% -> 2% of each run, Pallas kernels for 0% -> 0%
where the time goes in v3:
time: 119 us
  blocking collectives  79.7 us (67%)
  starting transfers between devices  19.4 us (16%)
  waiting for transfers between devices  8.69 us (7%)
  matrix products  3.85 us (3%)
  local copies, waits for them, and re-layouts  3.71 us (3%)
  other arithmetic  3.24 us (3%)
    all_to_all x3, blocking collectives, exchange(): return lax.all_to_all(blocks, axes, 0, 0, tiled=True)  52.2 us
    ppermute x4, starting transfers between devices, shift(): return lax.ppermute(block, 'y', [(i, (i + step) % 8) for i in range(8)])  15.3 us
    all_gather x1, blocking collectives, body(): halves = total(lax.all_gather(near, 'zh', axis=0))  13.5 us
    all_gather x1, blocking collectives, body(): given = lax.all_gather(give, 'c', axis=0)  9.85 us
    ppermute x4, waiting for transfers between devices, shift(): return lax.ppermute(block, 'y', [(i, (i + step) % 8) for i in range(8)])  7.92 us
    all_gather x1, blocking collectives, body(): out = lax.all_gather(out_half, 'c', axis=1, tiled=True)  4.26 us
    ppermute x1, starting transfers between devices, shift_by_core(): return lax.ppermute(block, ('y', 'c'), pairs)  4.16 us
    dot_general x2, matrix products, project(): lax.dot_general(rows, weight, (((1,), (1,)), ((), ())), preferred_element...  3.08 us
  transfers between devices with their start and end apart: 5, of which 4 were waited for; matrix products, arithmetic and copies ran while one was open for 2% of the time, Pallas kernels for 0%

profile of v3, /device:TPU:1, one launch (start us, length us, event | category | flops | bytes accessed | tf_op | source)
XLA Modules:
  0.0 118.8 jit_solution(7237175897045937030)
XLA Ops:
  0.0 0.0 copy-start
  0.0 1.3 %copy-done = bf16[832,768]{1,0:T(8,128)(2,1)S(1)} copy-done((bf16[832,768]{1,0:T(8,128)(2,1)S(1)}, bf16[832,768]{1,0:T(8,128)(2,1)}, u32[]{:S(2)}) %copy-start) | copy-done | bytes 1277976
  1.3 0.0 copy-start.3
  1.3 0.0 copy-start.5
  1.3 2.0 %fusion.17 = f32[384,832]{1,0:T(8,128)S(1)} fusion(bf16[832,768]{1,0:T(8,128)(2,1)S(1)} %copy-done, s32[]{:T(128)S(6)} %select_n.39, bf16[384,768]{1,0:T(8,128)(2,1)} %bitcast.42), kind=kOutput, calls=%fused_computation.44 | convolution fusion | flops 491913216 | bytes 3145732 | tf_op jit(solution)/shard_map/dot_general | solution.py:10
  3.3 0.0 copy-done.3
  3.3 0.0 copy-done.5
  3.4 1.1 fusion.19
  4.4 0.0 copy-start.1
  4.4 0.3 fusion
  4.8 0.8 copy-done.1
  5.5 0.7 slice_bitcast_fusion.7
  6.3 5.9 %collective-permute-start.1 = (bf16[2,48,1664]{2,1,0:T(8,128)(2,1)S(1)}, bf16[2,48,1664]{2,1,0:T(8,128)(2,1)}, u32[]{:S(2)}, u32[]{:S(2)}) collective-permute-start(bf16[2,48,1664]{2,1,0:T(8,128)(2,1)S(1)} %pad_maximum_fusion.2), channel_id=1, source_target_pairs={{0,448},{64,0},{128,64},{192,128},{256,192},{320,256},{384,320},{4... | collective-permute-start | bytes 958472 | tf_op jit(solution)/shard_map/ppermute | solution.py:26
  12.3 1.9 %collective-permute-start = (bf16[2,48,1664]{2,1,0:T(8,128)(2,1)S(1)}, bf16[2,48,1664]{2,1,0:T(8,128)(2,1)}, u32[]{:S(2)}, u32[]{:S(2)}) collective-permute-start(bf16[2,48,1664]{2,1,0:T(8,128)(2,1)S(1)} %pad_maximum_fusion.1), channel_id=1, source_target_pairs={{0,64},{64,128},{128,192},{192,256},{256,320},{320,384},{384,448},... | collective-permute-start | bytes 958472 | tf_op jit(solution)/shard_map/ppermute | solution.py:26
  14.2 4.2 %collective-permute-start.2 = (bf16[48,1664]{1,0:T(8,128)(2,1)}, bf16[48,1664]{1,0:T(8,128)(2,1)S(1)}, u32[]{:S(2)}, u32[]{:S(2)}) collective-permute-start(bf16[48,1664]{1,0:T(8,128)(2,1)} %get-tuple-element.10), channel_id=1, source_target_pairs={{0,128},{1,385},{64,192},{65,449},{128,256},{129,1},{192,320},{193... | collective-permute-start | bytes 479240 | tf_op jit(solution)/shard_map/ppermute | solution.py:34
  18.4 0.0 copy-start.2
  18.4 0.0 collective-permute-done.1
  18.4 1.1 convert_element_type.73
  19.5 2.1 %collective-permute-done = bf16[2,48,1664]{2,1,0:T(8,128)(2,1)} collective-permute-done((bf16[2,48,1664]{2,1,0:T(8,128)(2,1)S(1)}, bf16[2,48,1664]{2,1,0:T(8,128)(2,1)}, u32[]{:S(2)}, u32[]{:S(2)}) %collective-permute-start) | collective-permute-done | bytes 319520 | tf_op jit(solution)/shard_map/ppermute | solution.py:26
  21.7 1.0 convert_element_type.70
  22.7 0.8 collective-permute-done.2
  23.5 0.0 copy-done.2
  23.5 0.2 fusion.4
  23.6 4.5 %collective-permute-start.3 = (bf16[48,1664]{1,0:T(8,128)(2,1)S(1)}, bf16[48,1664]{1,0:T(8,128)(2,1)S(1)}, u32[]{:S(2)}, u32[]{:S(2)}) collective-permute-start(bf16[48,1664]{1,0:T(8,128)(2,1)S(1)} %get-tuple-element.7), channel_id=1, source_target_pairs={{0,128},{64,192},{128,256},{192,320},{256,384},{320,448},{384,0},{... | collective-permute-start | bytes 479240 | tf_op jit(solution)/shard_map/ppermute | solution.py:26
  28.2 2.8 %collective-permute-start.4 = (bf16[48,1664]{1,0:T(8,128)(2,1)S(1)}, bf16[48,1664]{1,0:T(8,128)(2,1)S(1)}, u32[]{:S(2)}, u32[]{:S(2)}) collective-permute-start(bf16[48,1664]{1,0:T(8,128)(2,1)S(1)} %get-tuple-element.8), channel_id=1, source_target_pairs={{0,384},{64,448},{128,0},{192,64},{256,128},{320,192},{384,256},{4... | collective-permute-start | bytes 479240 | tf_op jit(solution)/shard_map/ppermute | solution.py:26
  31.0 0.8 collective-permute-done.3
  31.9 5.0 %collective-permute-done.4 = bf16[48,1664]{1,0:T(8,128)(2,1)S(1)} collective-permute-done((bf16[48,1664]{1,0:T(8,128)(2,1)S(1)}, bf16[48,1664]{1,0:T(8,128)(2,1)S(1)}, u32[]{:S(2)}, u32[]{:S(2)}) %collective-permute-start.4) | collective-permute-done | bytes 159776 | tf_op jit(solution)/shard_map/ppermute | solution.py:26
  36.8 0.1 fusion.21
  36.9 13.5 %all-gather = bf16[96,1664]{1,0:T(8,128)(2,1)S(1)} all-gather(bf16[48,1664]{1,0:T(8,128)(2,1)S(1)} %get-tuple-element.5), channel_id=2, replica_groups=mesh['y'=8,'zh'=2,'zl'=4,'x'=4,'c'=2] {'zh'}, dimensions={0}, use_global_device_ids=true | all-gather | bytes 479232 | tf_op jit(solution)/shard_map/all_gather | solution.py:62
  50.5 0.1 subtract_add_fusion
  50.5 0.0 copy-start.4
  50.5 0.1 fusion.16
  50.6 0.1 broadcast_in_dim.11
  50.7 17.4 %all_to_all.15 = bf16[8,48,832]{2,1,0:T(8,128)(2,1)S(1)} all-to-all(bf16[8,48,832]{2,1,0:T(8,128)(2,1)S(1)} %broadcast_in_dim.11), channel_id=1, replica_groups=mesh['y'=8,'zh'=2,'zl'=4,'x'=4,'c'=2] {'y'}, dimensions={0} | all-to-all | bytes 1277952 | tf_op jit(solution)/shard_map/all_to_all | solution.py:14
  68.1 0.0 copy-done.4
  68.1 0.8 fusion.23
  68.9 0.1 select_convert_fusion
  69.0 9.8 %all-gather.1 = bf16[768,384]{1,0:T(8,128)(2,1)S(1)} all-gather(bf16[384,384]{1,0:T(8,128)(2,1)S(1)} %select_convert_fusion), channel_id=3, replica_groups=mesh['y'=8,'zh'=2,'zl'=4,'x'=4,'c'=2] {'c'}, dimensions={0}, use_global_device_ids=true | all-gather | bytes 884736 | tf_op jit(solution)/shard_map/all_gather | solution.py:72
  78.8 0.1 fusion.2
  78.9 20.7 %all_to_all.16 = bf16[16,24,384]{2,1,0:T(8,128)(2,1)S(1)} all-to-all(bf16[16,24,384]{2,1,0:T(8,128)(2,1)S(1)} %bitcast.39), channel_id=1, replica_groups=mesh['y'=8,'zh'=2,'zl'=4,'x'=4,'c'=2] {'zl','x'}, dimensions={0} | all-to-all | bytes 589824 | tf_op jit(solution)/shard_map/all_to_all | solution.py:14
  99.8 14.0 %all_to_all.17 = bf16[16,24,384]{2,1,0:T(8,128)(2,1)S(1)} all-to-all(bf16[16,24,384]{2,1,0:T(8,128)(2,1)S(1)} %broadcast_in_dim.20), channel_id=1, replica_groups=mesh['y'=8,'zh'=2,'zl'=4,'x'=4,'c'=2] {'zl','x'}, dimensions={0} | all-to-all | bytes 589824 | tf_op jit(solution)/shard_map/all_to_all | solution.py:14
  113.8 4.3 %all_gather.19 = bf16[384,768]{1,0:T(8,128)(2,1)S(1)} all-gather(bf16[384,384]{1,0:T(8,128)(2,1)S(1)} %bitcast.40), channel_id=1, replica_groups=mesh['y'=8,'zh'=2,'zl'=4,'x'=4,'c'=2] {'c'}, dimensions={1}, use_global_device_ids=true | all-gather | bytes 884736 | tf_op jit(solution)/shard_map/all_gather | solution.py:77
  118.0 0.8 copy.22
  (5 shorter events, 0.2 us)
Async XLA Ops:
  0.0 1.3 %copy-start = (bf16[832,768]{1,0:T(8,128)(2,1)S(1)}, bf16[832,768]{1,0:T(8,128)(2,1)}, u32[]{:S(2)}) copy-start(bf16[832,768]{1,0:T(8,128)(2,1)} %param.5) | copy-start | bytes 3833860
  1.3 2.0 %copy-start.3 = (bf16[832,768]{1,0:T(8,128)(2,1)S(1)}, bf16[832,768]{1,0:T(8,128)(2,1)}, u32[]{:S(2)}) copy-start(bf16[832,768]{1,0:T(8,128)(2,1)} %param.6) | copy-start | bytes 3833860
  1.3 2.0 %copy-start.5 = (bf16[2,192,768]{2,1,0:T(8,128)(2,1)S(1)}, bf16[2,192,768]{2,1,0:T(8,128)(2,1)}, u32[]{:S(2)}) copy-start(bf16[2,192,768]{2,1,0:T(8,128)(2,1)} %param.4) | copy-start | bytes 1769476
  4.4 1.1 copy-start.1
  6.3 12.1 %collective-permute-start.1 = (bf16[2,48,1664]{2,1,0:T(8,128)(2,1)S(1)}, bf16[2,48,1664]{2,1,0:T(8,128)(2,1)}, u32[]{:S(2)}, u32[]{:S(2)}) collective-permute-start(bf16[2,48,1664]{2,1,0:T(8,128)(2,1)S(1)} %pad_maximum_fusion.2), channel_id=1, source_target_pairs={{0,448},{64,0},{128,64},{192,128},{256,192},{320,256},{384,320},{4... | collective-permute-start | bytes 958472 | tf_op jit(solution)/shard_map/ppermute | solution.py:26
  12.3 9.4 %collective-permute-start = (bf16[2,48,1664]{2,1,0:T(8,128)(2,1)S(1)}, bf16[2,48,1664]{2,1,0:T(8,128)(2,1)}, u32[]{:S(2)}, u32[]{:S(2)}) collective-permute-start(bf16[2,48,1664]{2,1,0:T(8,128)(2,1)S(1)} %pad_maximum_fusion.1), channel_id=1, source_target_pairs={{0,64},{64,128},{128,192},{192,256},{256,320},{320,384},{384,448},... | collective-permute-start | bytes 958472 | tf_op jit(solution)/shard_map/ppermute | solution.py:26
  14.2 9.2 %collective-permute-start.2 = (bf16[48,1664]{1,0:T(8,128)(2,1)}, bf16[48,1664]{1,0:T(8,128)(2,1)S(1)}, u32[]{:S(2)}, u32[]{:S(2)}) collective-permute-start(bf16[48,1664]{1,0:T(8,128)(2,1)} %get-tuple-element.10), channel_id=1, source_target_pairs={{0,128},{1,385},{64,192},{65,449},{128,256},{129,1},{192,320},{193... | collective-permute-start | bytes 479240 | tf_op jit(solution)/shard_map/ppermute | solution.py:34
  18.4 5.1 %copy-start.2 = (f32[384,832]{1,0:T(8,128)S(1)}, f32[384,832]{1,0:T(8,128)}, u32[]{:S(2)}) copy-start(f32[384,832]{1,0:T(8,128)} %copy-done.1) | copy-start | bytes 3833860
  23.6 8.2 %collective-permute-start.3 = (bf16[48,1664]{1,0:T(8,128)(2,1)S(1)}, bf16[48,1664]{1,0:T(8,128)(2,1)S(1)}, u32[]{:S(2)}, u32[]{:S(2)}) collective-permute-start(bf16[48,1664]{1,0:T(8,128)(2,1)S(1)} %get-tuple-element.7), channel_id=1, source_target_pairs={{0,128},{64,192},{128,256},{192,320},{256,384},{320,448},{384,0},{... | collective-permute-start | bytes 479240 | tf_op jit(solution)/shard_map/ppermute | solution.py:26
  28.2 8.6 %collective-permute-start.4 = (bf16[48,1664]{1,0:T(8,128)(2,1)S(1)}, bf16[48,1664]{1,0:T(8,128)(2,1)S(1)}, u32[]{:S(2)}, u32[]{:S(2)}) collective-permute-start(bf16[48,1664]{1,0:T(8,128)(2,1)S(1)} %get-tuple-element.8), channel_id=1, source_target_pairs={{0,384},{64,448},{128,0},{192,64},{256,128},{320,192},{384,256},{4... | collective-permute-start | bytes 479240 | tf_op jit(solution)/shard_map/ppermute | solution.py:26
  50.5 17.6 %copy-start.4 = (bf16[832,768]{1,0:T(8,128)(2,1)S(1)}, bf16[832,768]{1,0:T(8,128)(2,1)}, u32[]{:S(2)}) copy-start(bf16[832,768]{1,0:T(8,128)(2,1)} %param.7) | copy-start | bytes 3833860

commit v4 on v3

v4 whole, which is shorter than its diff:
```python
import jax
import jax.numpy as jnp
from jax import lax
from jax.experimental import pallas as pl
from jax.experimental.pallas import tpu as pltpu
from jax.sharding import Mesh, PartitionSpec as P

PLANE = ("zl", "x")


ORDER = (4, 1, 3, 7, 5, 0, 2, 6)


def front_kernel(place, tokens, gate, up, far, ups, downs, keep, rows_in, weights, row_sems, weight_sems):
    chunk = rows_in.shape[0] // 8
    units = gate.shape[0]
    cut = units // 2
    loads = []
    for at, (source, start) in enumerate(((gate, 0), (gate, cut), (up, 0), (up, cut))):
        base = 0 if source is gate else units
        loads.append(
            pltpu.make_async_copy(
                source.at[pl.ds(start, cut)], weights.at[pl.ds(base + start, cut)], weight_sems.at[at]
            )
        )
    row_loads = []
    for at, ahead in enumerate(ORDER):
        row = lax.rem(place[0] + ahead, 8) * chunk
        row_loads.append(
            pltpu.make_async_copy(
                tokens.at[pl.ds(pl.multiple_of(row, chunk), chunk)],
                rows_in.at[pl.ds(at * chunk, chunk)],
                row_sems.at[at],
            )
        )
    loads[0].start()
    for load in row_loads:
        load.start()
    for load in loads[1:]:
        load.start()
    for load in row_loads:
        load.wait()
    ready = 0
    for start, stop, needs in ((0, 384, 1), (384, 768, 2), (768, 1152, 3), (1152, 1664, 4)):
        while ready < needs:
            loads[ready].wait()
            ready += 1
        out = lax.dot_general(
            rows_in[...],
            weights[start:stop, :],
            (((1,), (1,)), ((), ())),
            preferred_element_type=jnp.float32,
        )
        sent = out[: 5 * chunk].astype(jnp.bfloat16)
        far[:, start:stop] = sent[:chunk]
        for at in range(2):
            ups[at, :, start:stop] = sent[(1 + at) * chunk : (2 + at) * chunk]
            downs[at, :, start:stop] = sent[(3 + at) * chunk : (4 + at) * chunk]
        for at in range(3):
            keep[at, :, start:stop] = out[(5 + at) * chunk : (6 + at) * chunk]


def front(flat, gate_weight, up_weight):
    rows, width = flat.shape
    units = 2 * gate_weight.shape[0]
    chunk = rows // 8
    place = lax.axis_index("y").astype(jnp.int32).reshape(1)
    whole = pl.BlockSpec(memory_space=pl.ANY)
    vmem = pl.BlockSpec(memory_space=pltpu.VMEM)
    return pl.pallas_call(
        front_kernel,
        out_shape=(
            jax.ShapeDtypeStruct((chunk, units), jnp.bfloat16),
            jax.ShapeDtypeStruct((2, chunk, units), jnp.bfloat16),
            jax.ShapeDtypeStruct((2, chunk, units), jnp.bfloat16),
            jax.ShapeDtypeStruct((3, chunk, units), jnp.float32),
        ),
        in_specs=[pl.BlockSpec(memory_space=pltpu.SMEM), whole, whole, whole],
        out_specs=(vmem, vmem, vmem, vmem),
        scratch_shapes=[
            pltpu.VMEM((rows, width), jnp.bfloat16),
            pltpu.VMEM((units, width), jnp.bfloat16),
            pltpu.SemaphoreType.DMA((8,)),
            pltpu.SemaphoreType.DMA((4,)),
        ],
        compiler_params=pltpu.CompilerParams(vmem_limit_bytes=32 * 1024 * 1024),
        cost_estimate=pl.CostEstimate(
            flops=2 * rows * width * units, bytes_accessed=2 * width * (rows + units), transcendentals=0
        ),
    )(place, flat, gate_weight, up_weight)


def exchange(blocks, axes):
    return lax.all_to_all(blocks, axes, 0, 0, tiled=True)


def spread(block, axes, count):
    return exchange(jnp.broadcast_to(block[None], (count, *block.shape)), axes)


def total(blocks):
    return jnp.sum(blocks.astype(jnp.float32), axis=0)


def shift(block, step):
    return lax.ppermute(block, "y", [(i, (i + step) % 8) for i in range(8)])


def shift_by_core(block, step):
    pairs = []
    for i in range(8):
        pairs.append((2 * i, 2 * ((i + step) % 8)))
        pairs.append((2 * i + 1, 2 * ((i - step) % 8) + 1))
    return lax.ppermute(block, ("y", "c"), pairs)


def scatter_sum(far, ups, downs, keep):
    wide = jnp.float32
    first_core = lax.axis_index("c") == 0
    far = shift_by_core(far, 2)
    up = shift(ups, 1)
    down = shift(downs, -1)
    zero = jnp.zeros((), wide)
    up_two = keep[1] + up[1].astype(wide) + jnp.where(first_core, far.astype(wide), zero)
    down_two = keep[2] + down[1].astype(wide) + jnp.where(first_core, zero, far.astype(wide))
    last_up = shift(up_two.astype(jnp.bfloat16), 2)
    last_down = shift(down_two.astype(jnp.bfloat16), -2)
    return keep[0] + up[0].astype(wide) + down[0].astype(wide) + last_up.astype(wide) + last_down.astype(wide)


def body(tokens, gate_weight, up_weight, down_weight):
    steps, batch, width = tokens.shape
    rows = steps * batch
    local_ff = gate_weight.shape[0]
    flat = tokens.reshape(rows, width)
    y_sum = scatter_sum(*front(flat, gate_weight, up_weight))
    near = y_sum.astype(jnp.bfloat16)
    halves = total(lax.all_gather(near, "zh", axis=0))
    summed = halves + (y_sum - near.astype(jnp.float32))
    share = (jax.nn.silu(summed[:, :local_ff]) * summed[:, local_ff:]).astype(jnp.bfloat16)
    hidden = spread(share, "y", 8).reshape(rows, local_ff)
    partial_out = jnp.dot(hidden, down_weight, preferred_element_type=jnp.float32)

    half = width // 2
    first_core = lax.axis_index("c") == 0
    own = jnp.where(first_core, partial_out[:, :half], partial_out[:, half:])
    give = jnp.where(first_core, partial_out[:, half:], partial_out[:, :half])
    given = lax.all_gather(give, "c", axis=0)
    chip = own + jnp.where(first_core, given[1], given[0])
    chip = chip.astype(jnp.bfloat16).reshape(16, rows // 16, half)
    out_share = total(exchange(chip, PLANE)).astype(jnp.bfloat16)
    out_half = spread(out_share, PLANE, 16).reshape(rows, half)
    out = lax.all_gather(out_half, "c", axis=1, tiled=True)
    return out.reshape(steps, batch, width)


def solution(mesh):
    fine = Mesh(mesh.devices.reshape(8, 2, 4, 4, 2), ("y", "zh", "zl", "x", "c"))
    gx, gy = ("y", "zh"), ("zl", "x", "c")
    in_specs = (P(None, None, gx), P(gy, gx), P(gy, gx), P(gy, gx))
    return jax.shard_map(body, mesh=fine, in_specs=in_specs, out_specs=P(None, None, gx), check_vma=False)
```

time: 119 us -> 157 us (1.32)
  waiting for transfers between devices: 8.69 us -> 35.2 us
  between operations: 0.2 us -> 13.5 us
  blocking collectives: 79.7 us -> 71.5 us
  Pallas kernels: 0 us -> 3.62 us
  matrix products: 3.85 us -> 0.77 us
  other arithmetic: 3.24 us -> 5.54 us
  starting transfers between devices: 19.4 us -> 21.4 us
    all_gather x0 -> x1, waiting for transfers between devices: none -> 19.5 us  [body(): given = lax.all_gather(give, 'c', axis=0)]
    all_gather x1 -> x0, blocking collectives: 9.85 us -> none  [body(): given = lax.all_gather(give, 'c', axis=0)]
    ppermute x1, waiting for transfers between devices: 0.78 us -> 6.72 us  [shift_by_core(): return lax.ppermute(block, ('y', 'c'), pairs)]
    pallas_call x0 -> x1, Pallas kernels: none -> 3.62 us  [front(): pl.pallas_call(front_kernel, out_shape=(jax.ShapeDtypeStruct((chunk, unit...]
    dot_general x2 -> x0, matrix products: 3.08 us -> none  [project(): lax.dot_general(rows, weight, (((1,), (1,)), ((), ())), preferred_element...]
    convert_element_type x3 -> x0, other arithmetic: 2.19 us -> none  [the longest x1 1.12 us: scatter_sum(): down = shift(jnp.stack((sent[7], sent[5])), -1).astype(jnp.float32)]
    ppermute x4, starting transfers between devices: 15.3 us -> 17.3 us  [shift(): return lax.ppermute(block, 'y', [(i, (i + step) % 8) for i in range(8)])]
    unnamed x13 -> x9, local copies, waits for them, and re-layouts: 2.91 us -> 4.59 us
  transfers between devices with their start and end apart: 5 -> 6, of which waited for: 4 -> 4; matrix products, arithmetic and copies ran while one was open for 2% -> 0% of each run, Pallas kernels for 0% -> 0%
where the time goes in v4:
time: 157 us; the launch traced here: 156 us
  blocking collectives  71.5 us (46%)
  waiting for transfers between devices  35.2 us (22%)
  starting transfers between devices  21.4 us (14%)
  between operations  13.5 us (9%)
  other arithmetic  5.54 us (4%)
  local copies, waits for them, and re-layouts  4.67 us (3%)
  Pallas kernels  3.62 us (2%)
    all_to_all x3, blocking collectives, exchange(): return lax.all_to_all(blocks, axes, 0, 0, tiled=True)  52.6 us
    all_gather x1, waiting for transfers between devices, body(): given = lax.all_gather(give, 'c', axis=0)  19.5 us
    ppermute x4, starting transfers between devices, shift(): return lax.ppermute(block, 'y', [(i, (i + step) % 8) for i in range(8)])  17.3 us
    all_gather x1, blocking collectives, body(): halves = total(lax.all_gather(near, 'zh', axis=0))  14.7 us
    ppermute x4, waiting for transfers between devices, shift(): return lax.ppermute(block, 'y', [(i, (i + step) % 8) for i in range(8)])  8.97 us
    ppermute x1, waiting for transfers between devices, shift_by_core(): return lax.ppermute(block, ('y', 'c'), pairs)  6.72 us
    unnamed x9, local copies, waits for them, and re-layouts  4.59 us
    all_gather x1, blocking collectives, body(): out = lax.all_gather(out_half, 'c', axis=1, tiled=True)  4.23 us
  transfers between devices with their start and end apart: 6, of which 4 were waited for; matrix products, arithmetic and copies ran while one was open for 0% of the time, Pallas kernels for 0%

profile of v4, /device:TPU:1, one launch (start us, length us, event | category | flops | bytes accessed | tf_op | source)
XLA Modules:
  0.0 156.2 jit_solution(10820636296092271021)
XLA Ops:
  6.5 0.0 copy-start
  6.5 0.0 all-gather.4.cloned.1.call-start
  6.5 0.0 copy-start.1
  6.5 1.4 copy-done.1
  7.9 0.0 copy-start.2
  7.9 1.3 copy-done.2
  9.3 0.0 copy-start.3
  9.3 1.1 copy-done.3
  10.3 3.6 %shard_map.46 = (bf16[48,1664]{1,0:T(8,128)(2,1)S(1)}, bf16[2,48,1664]{2,1,0:T(8,128)(2,1)S(1)}, bf16[2,48,1664]{2,1,0:T(8,128)(2,1)S(1)}, f32[3,48,1664]{2,1,0:T(8,128)S(1)}) custom-call(s32[1]{0:T(128)} %bitcast.place, bf16[384,768]{1,0:T(8,128)(2,1)S(1)} %bitcast.22, bf16[832,768]{1,0:T(8,128)(2,1)S(1)} %copy-done.1, bf16[832,768]{1,0:T(8,128)(2,1)S(1)} %copy-done.2), custom_call_target="tpu_custom_call" | custom-call | flops 981467136 | bytes 3145728 | tf_op jit(solution)/shard_map/pallas_call | solution.py:70
  13.9 4.0 %collective-permute-start = (bf16[2,48,1664]{2,1,0:T(8,128)(2,1)S(1)}, bf16[2,48,1664]{2,1,0:T(8,128)(2,1)S(1)}, u32[]{:S(2)}, u32[]{:S(2)}) collective-permute-start(bf16[2,48,1664]{2,1,0:T(8,128)(2,1)S(1)} %get-tuple-element.10), channel_id=1, source_target_pairs={{0,64},{64,128},{128,192},{192,256},{256,320},{320,384},{384,448},... | collective-permute-start | bytes 958472 | tf_op jit(solution)/shard_map/ppermute | solution.py:106
  18.0 3.8 %collective-permute-start.1 = (bf16[2,48,1664]{2,1,0:T(8,128)(2,1)S(1)}, bf16[2,48,1664]{2,1,0:T(8,128)(2,1)}, u32[]{:S(2)}, u32[]{:S(2)}) collective-permute-start(bf16[2,48,1664]{2,1,0:T(8,128)(2,1)S(1)} %get-tuple-element.11), channel_id=1, source_target_pairs={{0,448},{64,0},{128,64},{192,128},{256,192},{320,256},{384,320},{4... | collective-permute-start | bytes 958472 | tf_op jit(solution)/shard_map/ppermute | solution.py:106
  21.8 4.1 %collective-permute-start.2 = (bf16[48,1664]{1,0:T(8,128)(2,1)S(1)}, bf16[48,1664]{1,0:T(8,128)(2,1)S(1)}, u32[]{:S(2)}, u32[]{:S(2)}) collective-permute-start(bf16[48,1664]{1,0:T(8,128)(2,1)S(1)} %get-tuple-element.12), channel_id=1, source_target_pairs={{0,128},{1,385},{64,192},{65,449},{128,256},{129,1},{192,320},{193... | collective-permute-start | bytes 479240 | tf_op jit(solution)/shard_map/ppermute | solution.py:114
  26.0 6.7 %collective-permute-done.2 = bf16[48,1664]{1,0:T(8,128)(2,1)S(1)} collective-permute-done((bf16[48,1664]{1,0:T(8,128)(2,1)S(1)}, bf16[48,1664]{1,0:T(8,128)(2,1)S(1)}, u32[]{:S(2)}, u32[]{:S(2)}) %collective-permute-start.2) | collective-permute-done | bytes 159776 | tf_op jit(solution)/shard_map/ppermute | solution.py:114
  32.7 0.0 collective-permute-done
  32.7 0.0 collective-permute-done.1
  32.7 1.0 fusion.3
  33.7 7.5 %collective-permute-start.3 = (bf16[48,1664]{1,0:T(8,128)(2,1)S(1)}, bf16[48,1664]{1,0:T(8,128)(2,1)S(1)}, u32[]{:S(2)}, u32[]{:S(2)}) collective-permute-start(bf16[48,1664]{1,0:T(8,128)(2,1)S(1)} %get-tuple-element.13), channel_id=1, source_target_pairs={{0,128},{64,192},{128,256},{192,320},{256,384},{320,448},{384,0},{... | collective-permute-start | bytes 479240 | tf_op jit(solution)/shard_map/ppermute | solution.py:106
  41.3 1.9 %collective-permute-start.4 = (bf16[48,1664]{1,0:T(8,128)(2,1)S(1)}, bf16[48,1664]{1,0:T(8,128)(2,1)S(1)}, u32[]{:S(2)}, u32[]{:S(2)}) collective-permute-start(bf16[48,1664]{1,0:T(8,128)(2,1)S(1)} %get-tuple-element.14), channel_id=1, source_target_pairs={{0,384},{64,448},{128,0},{192,64},{256,128},{320,192},{384,256},{4... | collective-permute-start | bytes 479240 | tf_op jit(solution)/shard_map/ppermute | solution.py:106
  43.2 4.0 %collective-permute-done.3 = bf16[48,1664]{1,0:T(8,128)(2,1)S(1)} collective-permute-done((bf16[48,1664]{1,0:T(8,128)(2,1)S(1)}, bf16[48,1664]{1,0:T(8,128)(2,1)S(1)}, u32[]{:S(2)}, u32[]{:S(2)}) %collective-permute-start.3) | collective-permute-done | bytes 159776 | tf_op jit(solution)/shard_map/ppermute | solution.py:106
  47.2 5.0 %collective-permute-done.4 = bf16[48,1664]{1,0:T(8,128)(2,1)S(1)} collective-permute-done((bf16[48,1664]{1,0:T(8,128)(2,1)S(1)}, bf16[48,1664]{1,0:T(8,128)(2,1)S(1)}, u32[]{:S(2)}, u32[]{:S(2)}) %collective-permute-start.4) | collective-permute-done | bytes 159776 | tf_op jit(solution)/shard_map/ppermute | solution.py:106
  52.2 1.0 fusion.8
  53.2 14.7 %all-gather = bf16[96,1664]{1,0:T(8,128)(2,1)S(1)} all-gather(bf16[48,1664]{1,0:T(8,128)(2,1)S(1)} %fusion.8), channel_id=2, replica_groups=mesh['y'=8,'zh'=2,'zl'=4,'x'=4,'c'=2] {'zh'}, dimensions={0}, use_global_device_ids=true | all-gather | bytes 479232 | tf_op jit(solution)/shard_map/all_gather | solution.py:138
  67.9 1.1 subtract_add_fusion
  69.0 0.1 fusion.7
  69.1 0.1 broadcast_in_dim.11
  69.2 22.0 %all_to_all.15 = bf16[8,48,832]{2,1,0:T(8,128)(2,1)S(1)} all-to-all(bf16[8,48,832]{2,1,0:T(8,128)(2,1)S(1)} %broadcast_in_dim.11), channel_id=1, replica_groups=mesh['y'=8,'zh'=2,'zl'=4,'x'=4,'c'=2] {'y'}, dimensions={0} | all-to-all | bytes 1277952 | tf_op jit(solution)/shard_map/all_to_all | solution.py:94
  91.2 0.0 copy-done
  91.2 0.8 fusion.9
  91.9 0.9 slice_select_fusion.1
  92.8 0.0 all-gather.4.cloned.1.call-update
  92.8 19.5 %all-gather.4.cloned.1.call-done = f32[768,384]{1,0:T(8,128)} async-done(((f32[384,384]{1,0:T(8,128)}), f32[768,384]{1,0:T(8,128)}) %all-gather.4.cloned.1.call-update) | async-done | bytes 1179664 | tf_op jit(solution)/shard_map/all_gather | solution.py:148
  112.3 1.3 fusion.1
  113.7 16.7 %all_to_all.16 = bf16[16,24,384]{2,1,0:T(8,128)(2,1)S(1)} all-to-all(bf16[16,24,384]{2,1,0:T(8,128)(2,1)S(1)} %bitcast.26), channel_id=1, replica_groups=mesh['y'=8,'zh'=2,'zl'=4,'x'=4,'c'=2] {'zl','x'}, dimensions={0} | all-to-all | bytes 589824 | tf_op jit(solution)/shard_map/all_to_all | solution.py:94
  130.4 14.0 %all_to_all.17 = bf16[16,24,384]{2,1,0:T(8,128)(2,1)S(1)} all-to-all(bf16[16,24,384]{2,1,0:T(8,128)(2,1)S(1)} %broadcast_in_dim.20), channel_id=1, replica_groups=mesh['y'=8,'zh'=2,'zl'=4,'x'=4,'c'=2] {'zl','x'}, dimensions={0} | all-to-all | bytes 589824 | tf_op jit(solution)/shard_map/all_to_all | solution.py:94
  144.4 4.2 %all_gather.19 = bf16[384,768]{1,0:T(8,128)(2,1)S(1)} all-gather(bf16[384,384]{1,0:T(8,128)(2,1)S(1)} %bitcast.25), channel_id=1, replica_groups=mesh['y'=8,'zh'=2,'zl'=4,'x'=4,'c'=2] {'c'}, dimensions={1}, use_global_device_ids=true | all-gather | bytes 884736 | tf_op jit(solution)/shard_map/all_gather | solution.py:153
  148.6 0.8 copy.6
  (3 shorter events, 0.1 us)
Async XLA Ops:
  6.5 84.6 %copy-start = (bf16[832,768]{1,0:T(8,128)(2,1)S(1)}, bf16[832,768]{1,0:T(8,128)(2,1)}, u32[]{:S(2)}) copy-start(bf16[832,768]{1,0:T(8,128)(2,1)} %param.7) | copy-start | bytes 3833860
  6.5 105.8 %all-gather.4.cloned.1.call-start = ((), (), s32[]{:S(2)}) async-start(), calls=%async_computation.3 | async-start | bytes 1769472 | tf_op jit(solution)/shard_map/all_gather | solution.py:148
  6.5 1.4 copy-start.1
  7.9 1.3 copy-start.2
  9.3 1.1 copy-start.3
  13.9 18.7 %collective-permute-start = (bf16[2,48,1664]{2,1,0:T(8,128)(2,1)S(1)}, bf16[2,48,1664]{2,1,0:T(8,128)(2,1)S(1)}, u32[]{:S(2)}, u32[]{:S(2)}) collective-permute-start(bf16[2,48,1664]{2,1,0:T(8,128)(2,1)S(1)} %get-tuple-element.10), channel_id=1, source_target_pairs={{0,64},{64,128},{128,192},{192,256},{256,320},{320,384},{384,448},... | collective-permute-start | bytes 958472 | tf_op jit(solution)/shard_map/ppermute | solution.py:106
  18.0 14.7 %collective-permute-start.1 = (bf16[2,48,1664]{2,1,0:T(8,128)(2,1)S(1)}, bf16[2,48,1664]{2,1,0:T(8,128)(2,1)}, u32[]{:S(2)}, u32[]{:S(2)}) collective-permute-start(bf16[2,48,1664]{2,1,0:T(8,128)(2,1)S(1)} %get-tuple-element.11), channel_id=1, source_target_pairs={{0,448},{64,0},{128,64},{192,128},{256,192},{320,256},{384,320},{4... | collective-permute-start | bytes 958472 | tf_op jit(solution)/shard_map/ppermute | solution.py:106
  21.8 10.9 %collective-permute-start.2 = (bf16[48,1664]{1,0:T(8,128)(2,1)S(1)}, bf16[48,1664]{1,0:T(8,128)(2,1)S(1)}, u32[]{:S(2)}, u32[]{:S(2)}) collective-permute-start(bf16[48,1664]{1,0:T(8,128)(2,1)S(1)} %get-tuple-element.12), channel_id=1, source_target_pairs={{0,128},{1,385},{64,192},{65,449},{128,256},{129,1},{192,320},{193... | collective-permute-start | bytes 479240 | tf_op jit(solution)/shard_map/ppermute | solution.py:114
  33.7 13.5 %collective-permute-start.3 = (bf16[48,1664]{1,0:T(8,128)(2,1)S(1)}, bf16[48,1664]{1,0:T(8,128)(2,1)S(1)}, u32[]{:S(2)}, u32[]{:S(2)}) collective-permute-start(bf16[48,1664]{1,0:T(8,128)(2,1)S(1)} %get-tuple-element.13), channel_id=1, source_target_pairs={{0,128},{64,192},{128,256},{192,320},{256,384},{320,448},{384,0},{... | collective-permute-start | bytes 479240 | tf_op jit(solution)/shard_map/ppermute | solution.py:106
  41.3 10.9 %collective-permute-start.4 = (bf16[48,1664]{1,0:T(8,128)(2,1)S(1)}, bf16[48,1664]{1,0:T(8,128)(2,1)S(1)}, u32[]{:S(2)}, u32[]{:S(2)}) collective-permute-start(bf16[48,1664]{1,0:T(8,128)(2,1)S(1)} %get-tuple-element.14), channel_id=1, source_target_pairs={{0,384},{64,448},{128,0},{192,64},{256,128},{320,192},{384,256},{4... | collective-permute-start | bytes 479240 | tf_op jit(solution)/shard_map/ppermute | solution.py:106
Sparse Core Ops, SparseCore 0:
  93.0 19.3 all-gather.3

commit v5 on v4

--- a/solution.py
+++ b/solution.py
@@ -65,7 +65,7 @@
     units = 2 * gate_weight.shape[0]
     chunk = rows // 8
     place = lax.axis_index("y").astype(jnp.int32).reshape(1)
-    whole = pl.BlockSpec(memory_space=pl.ANY)
+    whole = pl.BlockSpec(memory_space=pltpu.HBM)
     vmem = pl.BlockSpec(memory_space=pltpu.VMEM)
     return pl.pallas_call(
         front_kernel,
@@ -114,18 +114,72 @@
     return lax.ppermute(block, ("y", "c"), pairs)
 
 
+def small_call(kernel, out_shapes, *operands, smem=0, flops=0):
+    vmem = pl.BlockSpec(memory_space=pltpu.VMEM)
+    scalar = pl.BlockSpec(memory_space=pltpu.SMEM)
+    shapes = [jax.ShapeDtypeStruct(shape, dtype) for shape, dtype in out_shapes]
+    moved = sum(x.size * x.dtype.itemsize for x in operands[smem:]) + sum(
+        x.size * jnp.dtype(x.dtype).itemsize for x in shapes
+    )
+    return pl.pallas_call(
+        kernel,
+        out_shape=shapes,
+        in_specs=[scalar] * smem + [vmem] * (len(operands) - smem),
+        out_specs=[vmem] * len(shapes),
+        compiler_params=pltpu.CompilerParams(vmem_limit_bytes=24 * 1024 * 1024),
+        cost_estimate=pl.CostEstimate(flops=flops, bytes_accessed=moved, transcendentals=0),
+    )(*operands)
+
+
+def merge_kernel(core, far, up, down, keep, up_two, down_two, base):
+    wide = jnp.float32
+    to_up = jnp.where(core[0] == 0, 1.0, 0.0).astype(wide)
+    far_rows = far[...].astype(wide)
+    up_two[...] = (keep[1] + up[1].astype(wide) + far_rows * to_up).astype(jnp.bfloat16)
+    down_two[...] = (keep[2] + down[1].astype(wide) + far_rows * (1.0 - to_up)).astype(jnp.bfloat16)
+    base[...] = keep[0] + up[0].astype(wide) + down[0].astype(wide)
+
+
+def finish_kernel(base, last_up, last_down, near, rest):
+    wide = jnp.float32
+    y_sum = base[...] + last_up[...].astype(wide) + last_down[...].astype(wide)
+    rounded = y_sum.astype(jnp.bfloat16)
+    near[...] = rounded
+    rest[...] = y_sum - rounded.astype(wide)
+
+
+def activate_kernel(halves, rest, spread_out):
+    wide = jnp.float32
+    rows, units = spread_out.shape[1:]
+    summed = rest[...] + halves[:rows].astype(wide) + halves[rows:].astype(wide)
+    gate = summed[:, :units]
+    hidden = (gate / (1.0 + jnp.exp(-gate)) * summed[:, units:]).astype(jnp.bfloat16)
+    for at in range(spread_out.shape[0]):
+        spread_out[at] = hidden
+
+
+def down_kernel(hidden, weight, out):
+    blocks, rows, units = hidden.shape
+    left = hidden[...].reshape(blocks * rows, units)
+    half = out.shape[2]
+    for at in range(2):
+        out[at] = jnp.dot(left, weight[:, at * half : (at + 1) * half], preferred_element_type=jnp.float32)
+
+
 def scatter_sum(far, ups, downs, keep):
-    wide = jnp.float32
-    first_core = lax.axis_index("c") == 0
+    core = lax.axis_index("c").astype(jnp.int32).reshape(1)
     far = shift_by_core(far, 2)
     up = shift(ups, 1)
     down = shift(downs, -1)
-    zero = jnp.zeros((), wide)
-    up_two = keep[1] + up[1].astype(wide) + jnp.where(first_core, far.astype(wide), zero)
-    down_two = keep[2] + down[1].astype(wide) + jnp.where(first_core, zero, far.astype(wide))
-    last_up = shift(up_two.astype(jnp.bfloat16), 2)
-    last_down = shift(down_two.astype(jnp.bfloat16), -2)
-    return keep[0] + up[0].astype(wide) + down[0].astype(wide) + last_up.astype(wide) + last_down.astype(wide)
+    one = far.shape
+    up_two, down_two, base = small_call(
+        merge_kernel,
+        ((one, jnp.bfloat16), (one, jnp.bfloat16), (one, jnp.float32)),
+        core, far, up, down, keep, smem=1,
+    )
+    last_up = shift(up_two, 2)
+    last_down = shift(down_two, -2)
+    return small_call(finish_kernel, ((one, jnp.bfloat16), (one, jnp.float32)), base, last_up, last_down)
 
 
 def body(tokens, gate_weight, up_weight, down_weight):
@@ -133,20 +187,18 @@
     rows = steps * batch
     local_ff = gate_weight.shape[0]
     flat = tokens.reshape(rows, width)
-    y_sum = scatter_sum(*front(flat, gate_weight, up_weight))
-    near = y_sum.astype(jnp.bfloat16)
-    halves = total(lax.all_gather(near, "zh", axis=0))
-    summed = halves + (y_sum - near.astype(jnp.float32))
-    share = (jax.nn.silu(summed[:, :local_ff]) * summed[:, local_ff:]).astype(jnp.bfloat16)
-    hidden = spread(share, "y", 8).reshape(rows, local_ff)
-    partial_out = jnp.dot(hidden, down_weight, preferred_element_type=jnp.float32)
-
+    near, rest = scatter_sum(*front(flat, gate_weight, up_weight))
+    halves = lax.all_gather(near, "zh", axis=0, tiled=True)
+    blocks = (8, rows // 8, local_ff)
+    (shares,) = small_call(activate_kernel, ((blocks, jnp.bfloat16),), halves, rest)
+    hidden = exchange(shares, "y")
     half = width // 2
-    first_core = lax.axis_index("c") == 0
-    own = jnp.where(first_core, partial_out[:, :half], partial_out[:, half:])
-    give = jnp.where(first_core, partial_out[:, half:], partial_out[:, :half])
-    given = lax.all_gather(give, "c", axis=0)
-    chip = own + jnp.where(first_core, given[1], given[0])
+    (partial_out,) = small_call(
+        down_kernel,
+        (((2, rows, half), jnp.float32),),
+        hidden, down_weight, flops=2 * rows * local_ff * width,
+    )
+    chip = total(exchange(partial_out, "c"))
     chip = chip.astype(jnp.bfloat16).reshape(16, rows // 16, half)
     out_share = total(exchange(chip, PLANE)).astype(jnp.bfloat16)
     out_half = spread(out_share, PLANE, 16).reshape(rows, half)

time: 157 us -> 128 us (0.82)
  waiting for transfers between devices: 35.2 us -> 15.6 us
  between operations: 13.5 us -> 0.1 us
  blocking collectives: 71.5 us -> 80.9 us
  other arithmetic: 5.54 us -> 0.11 us
    all_gather x1 -> x0, waiting for transfers between devices: 19.5 us -> none  [body(): given = lax.all_gather(give, 'c', axis=0)]
    all_to_all x3 -> x4, blocking collectives: 52.6 us -> 64.7 us  [exchange(): return lax.all_to_all(blocks, axes, 0, 0, tiled=True)]
    convert_element_type x4 -> x0, other arithmetic: 3.52 us -> none  [the longest x1 1.35 us: body(): chip = chip.astype(jnp.bfloat16).reshape(16, rows // 16, half)]
    all_gather x1, blocking collectives: 14.7 us -> 12 us  [body(): halves = lax.all_gather(near, 'zh', axis=0, tiled=True)]
  transfers between devices with their start and end apart: 6 -> 5, of which waited for: 4 -> 3; matrix products, arithmetic and copies ran while one was open for 0% -> 0% of each run, Pallas kernels for 0% -> 0%
where the time goes in v5:
time: 128 us
  blocking collectives  80.9 us (63%)
  starting transfers between devices  21.5 us (17%)
  waiting for transfers between devices  15.6 us (12%)
  Pallas kernels  4.95 us (4%)
  local copies, waits for them, and re-layouts  4.52 us (4%)
    all_to_all x4, blocking collectives, exchange(): return lax.all_to_all(blocks, axes, 0, 0, tiled=True)  64.7 us
    ppermute x4, starting transfers between devices, shift(): return lax.ppermute(block, 'y', [(i, (i + step) % 8) for i in range(8)])  17.3 us
    all_gather x1, blocking collectives, body(): halves = lax.all_gather(near, 'zh', axis=0, tiled=True)  12 us
    ppermute x4, waiting for transfers between devices, shift(): return lax.ppermute(block, 'y', [(i, (i + step) % 8) for i in range(8)])  8.98 us
    ppermute x1, waiting for transfers between devices, shift_by_core(): return lax.ppermute(block, ('y', 'c'), pairs)  6.67 us
    unnamed x9, local copies, waits for them, and re-layouts  4.49 us
    all_gather x1, blocking collectives, body(): out = lax.all_gather(out_half, 'c', axis=1, tiled=True)  4.26 us
    ppermute x1, starting transfers between devices, shift_by_core(): return lax.ppermute(block, ('y', 'c'), pairs)  4.16 us
  transfers between devices with their start and end apart: 5, of which 3 were waited for; matrix products, arithmetic and copies ran while one was open for 0% of the time, Pallas kernels for 0%

profile of v5, /device:TPU:1, one launch (start us, length us, event | category | flops | bytes accessed | tf_op | source)
XLA Modules:
  0.0 127.8 jit_solution(14470485710934330230)
XLA Ops:
  0.0 0.0 copy-start.1
  0.0 1.3 %copy-done.1 = bf16[832,768]{1,0:T(8,128)(2,1)S(1)} copy-done((bf16[832,768]{1,0:T(8,128)(2,1)S(1)}, bf16[832,768]{1,0:T(8,128)(2,1)}, u32[]{:S(2)}) %copy-start.1) | copy-done | bytes 1277976
  1.3 0.0 copy-start.2
  1.3 1.3 %copy-done.2 = bf16[832,768]{1,0:T(8,128)(2,1)S(1)} copy-done((bf16[832,768]{1,0:T(8,128)(2,1)S(1)}, bf16[832,768]{1,0:T(8,128)(2,1)}, u32[]{:S(2)}) %copy-start.2) | copy-done | bytes 1277976
  2.6 0.0 copy-start.3
  2.6 1.1 copy-done.3
  3.7 3.6 %shard_map.46 = (bf16[48,1664]{1,0:T(8,128)(2,1)S(1)}, bf16[2,48,1664]{2,1,0:T(8,128)(2,1)S(1)}, bf16[2,48,1664]{2,1,0:T(8,128)(2,1)S(1)}, f32[3,48,1664]{2,1,0:T(8,128)S(1)}) custom-call(s32[1]{0:T(128)} %bitcast.1.place, bf16[384,768]{1,0:T(8,128)(2,1)S(1)} %bitcast.6, bf16[832,768]{1,0:T(8,128)(2,1)S(1)} %copy-done.1, bf16[832,768]{1,0:T(8,128)(2,1)S(1)} %copy-done.2), custom_call_target="tpu_custom_call" | custom-call | flops 981467136 | bytes 3145728 | tf_op jit(solution)/shard_map/pallas_call | solution.py:70
  7.3 4.0 %collective-permute-start.1 = (bf16[2,48,1664]{2,1,0:T(8,128)(2,1)S(1)}, bf16[2,48,1664]{2,1,0:T(8,128)(2,1)S(1)}, u32[]{:S(2)}, u32[]{:S(2)}) collective-permute-start(bf16[2,48,1664]{2,1,0:T(8,128)(2,1)S(1)} %get-tuple-element.15), channel_id=1, source_target_pairs={{0,64},{64,128},{128,192},{192,256},{256,320},{320,384},{384,448},... | collective-permute-start | bytes 958472 | tf_op jit(solution)/shard_map/ppermute | solution.py:106
  11.3 3.8 %collective-permute-start.2 = (bf16[2,48,1664]{2,1,0:T(8,128)(2,1)S(1)}, bf16[2,48,1664]{2,1,0:T(8,128)(2,1)S(1)}, u32[]{:S(2)}, u32[]{:S(2)}) collective-permute-start(bf16[2,48,1664]{2,1,0:T(8,128)(2,1)S(1)} %get-tuple-element.16), channel_id=1, source_target_pairs={{0,448},{64,0},{128,64},{192,128},{256,192},{320,256},{384,320},{4... | collective-permute-start | bytes 958472 | tf_op jit(solution)/shard_map/ppermute | solution.py:106
  15.2 4.2 %collective-permute-start = (bf16[48,1664]{1,0:T(8,128)(2,1)S(1)}, bf16[48,1664]{1,0:T(8,128)(2,1)S(1)}, u32[]{:S(2)}, u32[]{:S(2)}) collective-permute-start(bf16[48,1664]{1,0:T(8,128)(2,1)S(1)} %get-tuple-element.14), channel_id=1, source_target_pairs={{0,128},{1,385},{64,192},{65,449},{128,256},{129,1},{192,320},{193... | collective-permute-start | bytes 479240 | tf_op jit(solution)/shard_map/ppermute | solution.py:114
  19.3 6.7 %collective-permute-done.far = bf16[48,1664]{1,0:T(8,128)(2,1)S(1)} collective-permute-done((bf16[48,1664]{1,0:T(8,128)(2,1)S(1)}, bf16[48,1664]{1,0:T(8,128)(2,1)S(1)}, u32[]{:S(2)}, u32[]{:S(2)}) %collective-permute-start) | collective-permute-done | bytes 159776 | tf_op jit(solution)/shard_map/ppermute | solution.py:114
  26.0 0.0 collective-permute-done.1.up
  26.0 0.0 collective-permute-done.2.down
  26.0 0.2 shard_map.47
  26.2 7.6 %collective-permute-start.3 = (bf16[48,1664]{1,0:T(8,128)(2,1)S(1)}, bf16[48,1664]{1,0:T(8,128)(2,1)S(1)}, u32[]{:S(2)}, u32[]{:S(2)}) collective-permute-start(bf16[48,1664]{1,0:T(8,128)(2,1)S(1)} %get-tuple-element.19), channel_id=1, source_target_pairs={{0,128},{64,192},{128,256},{192,320},{256,384},{320,448},{384,0},{... | collective-permute-start | bytes 479240 | tf_op jit(solution)/shard_map/ppermute | solution.py:106
  33.8 1.9 %collective-permute-start.4 = (bf16[48,1664]{1,0:T(8,128)(2,1)S(1)}, bf16[48,1664]{1,0:T(8,128)(2,1)S(1)}, u32[]{:S(2)}, u32[]{:S(2)}) collective-permute-start(bf16[48,1664]{1,0:T(8,128)(2,1)S(1)} %get-tuple-element.20), channel_id=1, source_target_pairs={{0,384},{64,448},{128,0},{192,64},{256,128},{320,192},{384,256},{4... | collective-permute-start | bytes 479240 | tf_op jit(solution)/shard_map/ppermute | solution.py:106
  35.7 4.0 %collective-permute-done.3.last_up = bf16[48,1664]{1,0:T(8,128)(2,1)S(1)} collective-permute-done((bf16[48,1664]{1,0:T(8,128)(2,1)S(1)}, bf16[48,1664]{1,0:T(8,128)(2,1)S(1)}, u32[]{:S(2)}, u32[]{:S(2)}) %collective-permute-start.3) | collective-permute-done | bytes 159776 | tf_op jit(solution)/shard_map/ppermute | solution.py:106
  39.7 5.0 %collective-permute-done.4.last_down = bf16[48,1664]{1,0:T(8,128)(2,1)S(1)} collective-permute-done((bf16[48,1664]{1,0:T(8,128)(2,1)S(1)}, bf16[48,1664]{1,0:T(8,128)(2,1)S(1)}, u32[]{:S(2)}, u32[]{:S(2)}) %collective-permute-start.4) | collective-permute-done | bytes 159776 | tf_op jit(solution)/shard_map/ppermute | solution.py:106
  44.7 0.1 shard_map.48
  44.8 12.0 %all_gather.6.halves = bf16[96,1664]{1,0:T(8,128)(2,1)S(1)} all-gather(bf16[48,1664]{1,0:T(8,128)(2,1)S(1)} %get-tuple-element.21), channel_id=1, replica_groups=mesh['y'=8,'zh'=2,'zl'=4,'x'=4,'c'=2] {'zh'}, dimensions={0}, use_global_device_ids=true | all-gather | bytes 479232 | tf_op jit(solution)/shard_map/all_gather | solution.py:191
  56.7 0.0 copy-start
  56.7 0.1 shard_map.49
  56.9 23.0 %all_to_all.20.hidden = bf16[8,48,832]{2,1,0:T(8,128)(2,1)S(1)} all-to-all(bf16[8,48,832]{2,1,0:T(8,128)(2,1)S(1)} %shard_map.49), channel_id=1, replica_groups=mesh['y'=8,'zh'=2,'zl'=4,'x'=4,'c'=2] {'y'}, dimensions={0} | all-to-all | bytes 1277952 | tf_op jit(solution)/shard_map/all_to_all | solution.py:94
  79.8 0.0 copy-done
  79.8 0.9 shard_map.50
  80.8 7.8 %all_to_all.21 = f32[2,384,384]{2,1,0:T(8,128)S(1)} all-to-all(f32[2,384,384]{2,1,0:T(8,128)S(1)} %shard_map.50), channel_id=1, replica_groups=mesh['y'=8,'zh'=2,'zl'=4,'x'=4,'c'=2] {'c'}, dimensions={0} | all-to-all | bytes 2359296 | tf_op jit(solution)/shard_map/all_to_all | solution.py:94
  88.5 0.1 reduce_sum.21
  88.6 20.0 %all_to_all.22 = bf16[16,24,384]{2,1,0:T(8,128)(2,1)S(1)} all-to-all(bf16[16,24,384]{2,1,0:T(8,128)(2,1)S(1)} %bitcast.9), channel_id=1, replica_groups=mesh['y'=8,'zh'=2,'zl'=4,'x'=4,'c'=2] {'zl','x'}, dimensions={0} | all-to-all | bytes 589824 | tf_op jit(solution)/shard_map/all_to_all | solution.py:94
  108.7 14.0 %all_to_all.23 = bf16[16,24,384]{2,1,0:T(8,128)(2,1)S(1)} all-to-all(bf16[16,24,384]{2,1,0:T(8,128)(2,1)S(1)} %broadcast_in_dim.2), channel_id=1, replica_groups=mesh['y'=8,'zh'=2,'zl'=4,'x'=4,'c'=2] {'zl','x'}, dimensions={0} | all-to-all | bytes 589824 | tf_op jit(solution)/shard_map/all_to_all | solution.py:94
  122.7 4.3 %all_gather.7 = bf16[384,768]{1,0:T(8,128)(2,1)S(1)} all-gather(bf16[384,384]{1,0:T(8,128)(2,1)S(1)} %bitcast.8), channel_id=1, replica_groups=mesh['y'=8,'zh'=2,'zl'=4,'x'=4,'c'=2] {'c'}, dimensions={1}, use_global_device_ids=true | all-gather | bytes 884736 | tf_op jit(solution)/shard_map/all_gather | solution.py:205
  126.9 0.8 copy.6
  (2 shorter events, 0.1 us)
Async XLA Ops:
  0.0 1.3 %copy-start.1 = (bf16[832,768]{1,0:T(8,128)(2,1)S(1)}, bf16[832,768]{1,0:T(8,128)(2,1)}, u32[]{:S(2)}) copy-start(bf16[832,768]{1,0:T(8,128)(2,1)} %gate.1) | copy-start | bytes 3833860
  1.3 1.3 %copy-start.2 = (bf16[832,768]{1,0:T(8,128)(2,1)S(1)}, bf16[832,768]{1,0:T(8,128)(2,1)}, u32[]{:S(2)}) copy-start(bf16[832,768]{1,0:T(8,128)(2,1)} %up.1) | copy-start | bytes 3833860
  2.6 1.1 copy-start.3
  7.3 18.7 %collective-permute-start.1 = (bf16[2,48,1664]{2,1,0:T(8,128)(2,1)S(1)}, bf16[2,48,1664]{2,1,0:T(8,128)(2,1)S(1)}, u32[]{:S(2)}, u32[]{:S(2)}) collective-permute-start(bf16[2,48,1664]{2,1,0:T(8,128)(2,1)S(1)} %get-tuple-element.15), channel_id=1, source_target_pairs={{0,64},{64,128},{128,192},{192,256},{256,320},{320,384},{384,448},... | collective-permute-start | bytes 958472 | tf_op jit(solution)/shard_map/ppermute | solution.py:106
  11.3 14.7 %collective-permute-start.2 = (bf16[2,48,1664]{2,1,0:T(8,128)(2,1)S(1)}, bf16[2,48,1664]{2,1,0:T(8,128)(2,1)S(1)}, u32[]{:S(2)}, u32[]{:S(2)}) collective-permute-start(bf16[2,48,1664]{2,1,0:T(8,128)(2,1)S(1)} %get-tuple-element.16), channel_id=1, source_target_pairs={{0,448},{64,0},{128,64},{192,128},{256,192},{320,256},{384,320},{4... | collective-permute-start | bytes 958472 | tf_op jit(solution)/shard_map/ppermute | solution.py:106
  15.2 10.8 %collective-permute-start = (bf16[48,1664]{1,0:T(8,128)(2,1)S(1)}, bf16[48,1664]{1,0:T(8,128)(2,1)S(1)}, u32[]{:S(2)}, u32[]{:S(2)}) collective-permute-start(bf16[48,1664]{1,0:T(8,128)(2,1)S(1)} %get-tuple-element.14), channel_id=1, source_target_pairs={{0,128},{1,385},{64,192},{65,449},{128,256},{129,1},{192,320},{193... | collective-permute-start | bytes 479240 | tf_op jit(solution)/shard_map/ppermute | solution.py:114
  26.2 13.5 %collective-permute-start.3 = (bf16[48,1664]{1,0:T(8,128)(2,1)S(1)}, bf16[48,1664]{1,0:T(8,128)(2,1)S(1)}, u32[]{:S(2)}, u32[]{:S(2)}) collective-permute-start(bf16[48,1664]{1,0:T(8,128)(2,1)S(1)} %get-tuple-element.19), channel_id=1, source_target_pairs={{0,128},{64,192},{128,256},{192,320},{256,384},{320,448},{384,0},{... | collective-permute-start | bytes 479240 | tf_op jit(solution)/shard_map/ppermute | solution.py:106
  33.8 10.9 %collective-permute-start.4 = (bf16[48,1664]{1,0:T(8,128)(2,1)S(1)}, bf16[48,1664]{1,0:T(8,128)(2,1)S(1)}, u32[]{:S(2)}, u32[]{:S(2)}) collective-permute-start(bf16[48,1664]{1,0:T(8,128)(2,1)S(1)} %get-tuple-element.20), channel_id=1, source_target_pairs={{0,384},{64,448},{128,0},{192,64},{256,128},{320,192},{384,256},{4... | collective-permute-start | bytes 479240 | tf_op jit(solution)/shard_map/ppermute | solution.py:106
  56.7 23.1 %copy-start = (bf16[832,768]{1,0:T(8,128)(2,1)S(1)}, bf16[832,768]{1,0:T(8,128)(2,1)}, u32[]{:S(2)}) copy-start(bf16[832,768]{1,0:T(8,128)(2,1)} %weight.1) | copy-start | bytes 3833860

commit v6 on v5

v6 whole, which is shorter than its diff:
```python
import jax
import jax.numpy as jnp
from jax import lax
from jax.experimental import pallas as pl
from jax.experimental.pallas import tpu as pltpu
from jax.sharding import Mesh, PartitionSpec as P

PLANE = ("x", "zl")


SENT = (4, 1, 3, 7, 5)
KEPT = (0, 2, 6)


def blocks_of(order, place, tokens, gate, up, rows_in, weights, row_sems, weight_sems):
    chunk = rows_in.shape[0] // len(order)
    units = gate.shape[0]
    loads = [
        pltpu.make_async_copy(source, weights.at[pl.ds(base, units)], weight_sems.at[at])
        for at, (source, base) in enumerate(((gate, 0), (up, units)))
    ]
    for at, ahead in enumerate(order):
        row = lax.rem(place[0] + ahead, 8) * chunk
        loads.append(
            pltpu.make_async_copy(
                tokens.at[pl.ds(pl.multiple_of(row, chunk), chunk)],
                rows_in.at[pl.ds(at * chunk, chunk)],
                row_sems.at[at],
            )
        )
    for load in loads:
        load.start()
    for load in loads:
        load.wait()
    return lax.dot_general(
        rows_in[...], weights[...], (((1,), (1,)), ((), ())), preferred_element_type=jnp.float32
    )


def send_kernel(place, tokens, gate, up, far, ups, downs, *scratch):
    chunk = far.shape[0]
    sent = blocks_of(SENT, place, tokens, gate, up, *scratch).astype(jnp.bfloat16)
    far[...] = sent[:chunk]
    for at in range(2):
        ups[at] = sent[(1 + at) * chunk : (2 + at) * chunk]
        downs[at] = sent[(3 + at) * chunk : (4 + at) * chunk]


def keep_kernel(place, tokens, gate, up, keep, *scratch):
    chunk = keep.shape[1]
    out = blocks_of(KEPT, place, tokens, gate, up, *scratch)
    for at in range(3):
        keep[at] = out[at * chunk : (at + 1) * chunk]


def front(flat, gate_weight, up_weight):
    rows, width = flat.shape
    units = 2 * gate_weight.shape[0]
    chunk = rows // 8
    place = lax.axis_index("y").astype(jnp.int32).reshape(1)
    whole = pl.BlockSpec(memory_space=pltpu.HBM)
    vmem = pl.BlockSpec(memory_space=pltpu.VMEM)

    def call(kernel, order, out_shapes):
        taken = len(order) * chunk
        return pl.pallas_call(
            kernel,
            out_shape=out_shapes,
            in_specs=[pl.BlockSpec(memory_space=pltpu.SMEM), whole, whole, whole],
            out_specs=[vmem] * len(out_shapes),
            scratch_shapes=[
                pltpu.VMEM((taken, width), jnp.bfloat16),
                pltpu.VMEM((units, width), jnp.bfloat16),
                pltpu.SemaphoreType.DMA((len(order),)),
                pltpu.SemaphoreType.DMA((2,)),
            ],
            compiler_params=pltpu.CompilerParams(vmem_limit_bytes=60 * 1024 * 1024),
            cost_estimate=pl.CostEstimate(
                flops=2 * taken * width * units,
                bytes_accessed=2 * width * (taken + units),
                transcendentals=0,
            ),
        )(place, flat, gate_weight, up_weight)

    one = jax.ShapeDtypeStruct((chunk, units), jnp.bfloat16)
    two = jax.ShapeDtypeStruct((2, chunk, units), jnp.bfloat16)
    far, ups, downs = call(send_kernel, SENT, [one, two, two])
    (keep,) = call(keep_kernel, KEPT, [jax.ShapeDtypeStruct((3, chunk, units), jnp.float32)])
    return far, ups, downs, keep


def exchange(blocks, axes):
    return lax.all_to_all(blocks, axes, 0, 0, tiled=True)


def spread(block, axes, count):
    return exchange(jnp.broadcast_to(block[None], (count, *block.shape)), axes)


def total(blocks):
    return jnp.sum(blocks.astype(jnp.float32), axis=0)


def shift(block, step):
    return lax.ppermute(block, "y", [(i, (i + step) % 8) for i in range(8)])


def shift_by_core(block, step):
    pairs = []
    for i in range(8):
        pairs.append((2 * i, 2 * ((i + step) % 8)))
        pairs.append((2 * i + 1, 2 * ((i - step) % 8) + 1))
    return lax.ppermute(block, ("y", "c"), pairs)


def small_call(kernel, out_shapes, *operands, smem=0, flops=0):
    vmem = pl.BlockSpec(memory_space=pltpu.VMEM)
    scalar = pl.BlockSpec(memory_space=pltpu.SMEM)
    shapes = [jax.ShapeDtypeStruct(shape, dtype) for shape, dtype in out_shapes]
    moved = sum(x.size * x.dtype.itemsize for x in operands[smem:]) + sum(
        x.size * jnp.dtype(x.dtype).itemsize for x in shapes
    )
    return pl.pallas_call(
        kernel,
        out_shape=shapes,
        in_specs=[scalar] * smem + [vmem] * (len(operands) - smem),
        out_specs=[vmem] * len(shapes),
        compiler_params=pltpu.CompilerParams(vmem_limit_bytes=24 * 1024 * 1024),
        cost_estimate=pl.CostEstimate(flops=flops, bytes_accessed=moved, transcendentals=0),
    )(*operands)


def merge_kernel(core, far, up, down, keep, down_two, up_two, base):
    wide = jnp.float32
    to_up = jnp.where(core[0] == 0, 0.0, 1.0).astype(wide)
    far_rows = far[...].astype(wide)
    up_two[...] = (keep[1] + up[1].astype(wide) + far_rows * to_up).astype(jnp.bfloat16)
    down_two[...] = (keep[2] + down[1].astype(wide) + far_rows * (1.0 - to_up)).astype(jnp.bfloat16)
    base[...] = keep[0] + up[0].astype(wide) + down[0].astype(wide)


def finish_kernel(base, last_up, last_down, near, rest):
    wide = jnp.float32
    y_sum = base[...] + last_up[...].astype(wide) + last_down[...].astype(wide)
    rounded = y_sum.astype(jnp.bfloat16)
    near[...] = rounded
    rest[...] = y_sum - rounded.astype(wide)


def activate_kernel(halves, rest, spread_out):
    wide = jnp.float32
    rows, units = spread_out.shape[1:]
    summed = rest[...] + halves[:rows].astype(wide) + halves[rows:].astype(wide)
    gate = summed[:, :units]
    hidden = (gate / (1.0 + jnp.exp(-gate)) * summed[:, units:]).astype(jnp.bfloat16)
    for at in range(spread_out.shape[0]):
        spread_out[at] = hidden


def down_kernel(core, hidden, weight, own, give):
    blocks, rows, units = hidden.shape
    left = hidden[...].reshape(blocks * rows, units)
    half = own.shape[1]
    mine = pl.ds(pl.multiple_of(core[0] * half, half), half)
    other = pl.ds(pl.multiple_of((1 - core[0]) * half, half), half)
    own[...] = jnp.dot(left, weight[:, mine], preferred_element_type=jnp.float32)
    give[...] = jnp.dot(left, weight[:, other], preferred_element_type=jnp.float32).astype(jnp.bfloat16)


def scatter_sum(far, ups, downs, keep):
    core = lax.axis_index("c").astype(jnp.int32).reshape(1)
    far = shift_by_core(far, -2)
    up = shift(ups, 1)
    down = shift(downs, -1)
    one = far.shape
    down_two, up_two, base = small_call(
        merge_kernel,
        ((one, jnp.bfloat16), (one, jnp.bfloat16), (one, jnp.float32)),
        core, far, up, down, keep, smem=1,
    )
    last_down = shift(down_two, -2)
    last_up = shift(up_two, 2)
    return small_call(finish_kernel, ((one, jnp.bfloat16), (one, jnp.float32)), base, last_down, last_up)


def body(tokens, gate_weight, up_weight, down_weight):
    steps, batch, width = tokens.shape
    rows = steps * batch
    local_ff = gate_weight.shape[0]
    flat = tokens.reshape(rows, width)
    near, rest = scatter_sum(*front(flat, gate_weight, up_weight))
    halves = lax.all_gather(near, "zh", axis=0, tiled=True)
    blocks = (8, rows // 8, local_ff)
    (shares,) = small_call(activate_kernel, ((blocks, jnp.bfloat16),), halves, rest)
    core = lax.axis_index("c").astype(jnp.int32)
    shares, core, first = lax.optimization_barrier((shares, core, core == 0))
    hidden = exchange(shares, "y")
    half = width // 2
    own, give = small_call(
        down_kernel,
        (((rows, half), jnp.float32), ((rows, half), jnp.bfloat16)),
        core.reshape(1), hidden, down_weight, smem=1, flops=2 * rows * local_ff * width,
    )
    given = lax.all_gather(give, "c", axis=0)
    chip = own + jnp.where(first, given[1], given[0]).astype(jnp.float32)
    chip = chip.astype(jnp.bfloat16).reshape(16, rows // 16, half)
    out_share = total(exchange(chip, PLANE)).astype(jnp.bfloat16)
    out_half = spread(out_share, PLANE, 16).reshape(rows, half)
    out = lax.all_gather(out_half, "c", axis=1, tiled=True)
    return out.reshape(steps, batch, width)


def solution(mesh):
    fine = Mesh(mesh.devices.reshape(8, 2, 4, 4, 2), ("y", "zh", "zl", "x", "c"))
    gx, gy = ("y", "zh"), ("zl", "x", "c")
    in_specs = (P(None, None, gx), P(gy, gx), P(gy, gx), P(gy, gx))
    return jax.shard_map(body, mesh=fine, in_specs=in_specs, out_specs=P(None, None, gx), check_vma=False)
```

time: 128 us -> 117 us (0.914)
  waiting for transfers between devices: 15.6 us -> 9.43 us
  starting transfers between devices: 21.5 us -> 16.5 us
  Pallas kernels: 4.95 us -> 8.6 us
  local copies, waits for them, and re-layouts: 4.52 us -> 2.04 us
  blocking collectives: 80.9 us -> 79.3 us
    all_to_all x4 -> x3, blocking collectives: 64.7 us -> 51.8 us  [exchange(): return lax.all_to_all(blocks, axes, 0, 0, tiled=True)]
    all_gather x0 -> x1, blocking collectives: none -> 10.1 us  [body(): given = lax.all_gather(give, 'c', axis=0)]
    pallas_call x1 -> x2, Pallas kernels: 3.62 us -> 7.27 us  [call(): pl.pallas_call(kernel, out_shape=out_shapes, in_specs=[pl.BlockSpec(memor...]
    ppermute x4, waiting for transfers between devices: 8.98 us -> 5.59 us  [shift(): return lax.ppermute(block, 'y', [(i, (i + step) % 8) for i in range(8)])]
    ppermute x4, starting transfers between devices: 17.3 us -> 14 us  [shift(): return lax.ppermute(block, 'y', [(i, (i + step) % 8) for i in range(8)])]
    ppermute x1, waiting for transfers between devices: 6.67 us -> 3.84 us  [shift_by_core(): return lax.ppermute(block, ('y', 'c'), pairs)]
    unnamed x9 -> x5, local copies, waits for them, and re-layouts: 4.49 us -> 2.01 us
    ppermute x1, starting transfers between devices: 4.16 us -> 2.48 us  [shift_by_core(): return lax.ppermute(block, ('y', 'c'), pairs)]
  transfers between devices with their start and end apart: 5 -> 5, of which waited for: 3 -> 3; matrix products, arithmetic and copies ran while one was open for 0% -> 0% of each run, Pallas kernels for 0% -> 3%
where the time goes in v6:
time: 117 us; the launch traced here: 116 us
  blocking collectives  79.3 us (68%)
  starting transfers between devices  16.5 us (14%)
  waiting for transfers between devices  9.43 us (8%)
  Pallas kernels  8.6 us (7%)
  local copies, waits for them, and re-layouts  2.04 us (2%)
    all_to_all x3, blocking collectives, exchange(): return lax.all_to_all(blocks, axes, 0, 0, tiled=True)  51.8 us
    ppermute x4, starting transfers between devices, shift(): return lax.ppermute(block, 'y', [(i, (i + step) % 8) for i in range(8)])  14 us
    all_gather x1, blocking collectives, body(): halves = lax.all_gather(near, 'zh', axis=0, tiled=True)  13.6 us
    all_gather x1, blocking collectives, body(): given = lax.all_gather(give, 'c', axis=0)  10.1 us
    pallas_call x2, Pallas kernels, call(): pl.pallas_call(kernel, out_shape=out_shapes, in_specs=[pl.BlockSpec(memor...  7.27 us
    ppermute x4, waiting for transfers between devices, shift(): return lax.ppermute(block, 'y', [(i, (i + step) % 8) for i in range(8)])  5.59 us
    ppermute x1, waiting for transfers between devices, shift_by_core(): return lax.ppermute(block, ('y', 'c'), pairs)  3.84 us
    all_gather x1, blocking collectives, body(): out = lax.all_gather(out_half, 'c', axis=1, tiled=True)  3.81 us
  transfers between devices with their start and end apart: 5, of which 3 were waited for; matrix products, arithmetic and copies ran while one was open for 0% of the time, Pallas kernels for 3%

profile of v6, /device:TPU:1, one launch (start us, length us, event | category | flops | bytes accessed | tf_op | source)
XLA Modules:
  0.0 116.2 jit_solution(9923169372765143092)
XLA Ops:
  0.0 3.6 %shard_map.46 = (bf16[48,1664]{1,0:T(8,128)(2,1)}, bf16[2,48,1664]{2,1,0:T(8,128)(2,1)}, bf16[2,48,1664]{2,1,0:T(8,128)(2,1)}) custom-call(s32[1]{0:T(128)} %bitcast.1.place, bf16[384,768]{1,0:T(8,128)(2,1)} %bitcast.8, bf16[832,768]{1,0:T(8,128)(2,1)} %gate.3, bf16[832,768]{1,0:T(8,128)(2,1)} %up.3), custom_call_target="tpu_custom_call" | custom-call | flops 613416960 | bytes 2924544 | tf_op jit(solution)/shard_map/pallas_call | solution.py:66
  3.6 4.0 %collective-permute-start.1 = (bf16[2,48,1664]{2,1,0:T(8,128)(2,1)}, bf16[2,48,1664]{2,1,0:T(8,128)(2,1)S(1)}, u32[]{:S(2)}, u32[]{:S(2)}) collective-permute-start(bf16[2,48,1664]{2,1,0:T(8,128)(2,1)} %get-tuple-element.19), channel_id=1, source_target_pairs={{0,64},{64,128},{128,192},{192,256},{256,320},{320,384},{384,448},... | collective-permute-start | bytes 958472 | tf_op jit(solution)/shard_map/ppermute | solution.py:105
  7.7 3.8 %collective-permute-start.2 = (bf16[2,48,1664]{2,1,0:T(8,128)(2,1)}, bf16[2,48,1664]{2,1,0:T(8,128)(2,1)S(1)}, u32[]{:S(2)}, u32[]{:S(2)}) collective-permute-start(bf16[2,48,1664]{2,1,0:T(8,128)(2,1)} %get-tuple-element.20), channel_id=1, source_target_pairs={{0,448},{64,0},{128,64},{192,128},{256,192},{320,256},{384,320},{4... | collective-permute-start | bytes 958472 | tf_op jit(solution)/shard_map/ppermute | solution.py:105
  11.5 2.5 %collective-permute-start = (bf16[48,1664]{1,0:T(8,128)(2,1)}, bf16[48,1664]{1,0:T(8,128)(2,1)S(1)}, u32[]{:S(2)}, u32[]{:S(2)}) collective-permute-start(bf16[48,1664]{1,0:T(8,128)(2,1)} %get-tuple-element.18), channel_id=1, source_target_pairs={{0,384},{1,129},{64,448},{65,193},{128,0},{129,257},{192,64},{193,... | collective-permute-start | bytes 479240 | tf_op jit(solution)/shard_map/ppermute | solution.py:113
  14.0 3.7 %shard_map.47.keep = f32[3,48,1664]{2,1,0:T(8,128)} custom-call(s32[1]{0:T(128)} %bitcast.1.place, bf16[384,768]{1,0:T(8,128)(2,1)} %bitcast.9, bf16[832,768]{1,0:T(8,128)(2,1)} %gate.3, bf16[832,768]{1,0:T(8,128)(2,1)} %up.3), custom_call_target="tpu_custom_call" | custom-call | flops 368050176 | bytes 2777088 | tf_op jit(solution)/shard_map/pallas_call | solution.py:66
  17.6 3.8 %collective-permute-done.far = bf16[48,1664]{1,0:T(8,128)(2,1)S(1)} collective-permute-done((bf16[48,1664]{1,0:T(8,128)(2,1)}, bf16[48,1664]{1,0:T(8,128)(2,1)S(1)}, u32[]{:S(2)}, u32[]{:S(2)}) %collective-permute-start) | collective-permute-done | bytes 159776 | tf_op jit(solution)/shard_map/ppermute | solution.py:113
  21.5 0.0 collective-permute-done.1.up
  21.5 0.0 collective-permute-done.2.down
  21.5 0.0 copy-start
  21.5 1.2 %copy-done = f32[3,48,1664]{2,1,0:T(8,128)S(1)} copy-done((f32[3,48,1664]{2,1,0:T(8,128)S(1)}, f32[3,48,1664]{2,1,0:T(8,128)}, u32[]{:S(2)}) %copy-start) | copy-done | bytes 958488
  22.7 0.2 shard_map.48
  22.9 3.6 %collective-permute-start.3 = (bf16[48,1664]{1,0:T(8,128)(2,1)S(1)}, bf16[48,1664]{1,0:T(8,128)(2,1)S(1)}, u32[]{:S(2)}, u32[]{:S(2)}) collective-permute-start(bf16[48,1664]{1,0:T(8,128)(2,1)S(1)} %get-tuple-element.22), channel_id=1, source_target_pairs={{0,384},{64,448},{128,0},{192,64},{256,128},{320,192},{384,256},{4... | collective-permute-start | bytes 479240 | tf_op jit(solution)/shard_map/ppermute | solution.py:105
  26.4 2.6 %collective-permute-start.4 = (bf16[48,1664]{1,0:T(8,128)(2,1)S(1)}, bf16[48,1664]{1,0:T(8,128)(2,1)S(1)}, u32[]{:S(2)}, u32[]{:S(2)}) collective-permute-start(bf16[48,1664]{1,0:T(8,128)(2,1)S(1)} %get-tuple-element.23), channel_id=1, source_target_pairs={{0,128},{64,192},{128,256},{192,320},{256,384},{320,448},{384,0},{... | collective-permute-start | bytes 479240 | tf_op jit(solution)/shard_map/ppermute | solution.py:105
  29.1 2.5 %collective-permute-done.3.last_up = bf16[48,1664]{1,0:T(8,128)(2,1)S(1)} collective-permute-done((bf16[48,1664]{1,0:T(8,128)(2,1)S(1)}, bf16[48,1664]{1,0:T(8,128)(2,1)S(1)}, u32[]{:S(2)}, u32[]{:S(2)}) %collective-permute-start.3) | collective-permute-done | bytes 159776 | tf_op jit(solution)/shard_map/ppermute | solution.py:105
  31.5 3.1 %collective-permute-done.4.last_down = bf16[48,1664]{1,0:T(8,128)(2,1)S(1)} collective-permute-done((bf16[48,1664]{1,0:T(8,128)(2,1)S(1)}, bf16[48,1664]{1,0:T(8,128)(2,1)S(1)}, u32[]{:S(2)}, u32[]{:S(2)}) %collective-permute-start.4) | collective-permute-done | bytes 159776 | tf_op jit(solution)/shard_map/ppermute | solution.py:105
  34.7 0.1 shard_map.49
  34.7 13.6 %all_gather.12.halves = bf16[96,1664]{1,0:T(8,128)(2,1)S(1)} all-gather(bf16[48,1664]{1,0:T(8,128)(2,1)S(1)} %get-tuple-element.24), channel_id=1, replica_groups=mesh['y'=8,'zh'=2,'zl'=4,'x'=4,'c'=2] {'zh'}, dimensions={0}, use_global_device_ids=true | all-gather | bytes 479232 | tf_op jit(solution)/shard_map/all_gather | solution.py:192
  48.3 0.0 copy-start.1
  48.3 0.1 shard_map.50
  48.5 19.5 %all_to_all.15.hidden = bf16[8,48,832]{2,1,0:T(8,128)(2,1)S(1)} all-to-all(bf16[8,48,832]{2,1,0:T(8,128)(2,1)S(1)} %shard_map.50), channel_id=1, replica_groups=mesh['y'=8,'zh'=2,'zl'=4,'x'=4,'c'=2] {'y'}, dimensions={0} | all-to-all | bytes 1277952 | tf_op jit(solution)/shard_map/all_to_all | solution.py:93
  67.9 0.0 copy-done.1
  67.9 0.9 shard_map.51
  68.9 10.1 %all-gather = bf16[768,384]{1,0:T(8,128)(2,1)S(1)} all-gather(bf16[384,384]{1,0:T(8,128)(2,1)S(1)} %get-tuple-element.30), channel_id=2, replica_groups=mesh['y'=8,'zh'=2,'zl'=4,'x'=4,'c'=2] {'c'}, dimensions={0}, use_global_device_ids=true | all-gather | bytes 884736 | tf_op jit(solution)/shard_map/all_gather | solution.py:204
  79.0 0.1 fusion
  79.1 18.1 %all_to_all.16 = bf16[16,24,384]{2,1,0:T(8,128)(2,1)S(1)} all-to-all(bf16[16,24,384]{2,1,0:T(8,128)(2,1)S(1)} %bitcast.11), channel_id=1, replica_groups=mesh['y'=8,'zh'=2,'zl'=4,'x'=4,'c'=2] {'x','zl'}, dimensions={0} | all-to-all | bytes 589824 | tf_op jit(solution)/shard_map/all_to_all | solution.py:93
  97.3 14.2 %all_to_all.17 = bf16[16,24,384]{2,1,0:T(8,128)(2,1)S(1)} all-to-all(bf16[16,24,384]{2,1,0:T(8,128)(2,1)S(1)} %broadcast_in_dim.2), channel_id=1, replica_groups=mesh['y'=8,'zh'=2,'zl'=4,'x'=4,'c'=2] {'x','zl'}, dimensions={0} | all-to-all | bytes 589824 | tf_op jit(solution)/shard_map/all_to_all | solution.py:93
  111.5 3.8 %all_gather.15 = bf16[384,768]{1,0:T(8,128)(2,1)S(1)} all-gather(bf16[384,384]{1,0:T(8,128)(2,1)S(1)} %bitcast.10), channel_id=1, replica_groups=mesh['y'=8,'zh'=2,'zl'=4,'x'=4,'c'=2] {'c'}, dimensions={1}, use_global_device_ids=true | all-gather | bytes 884736 | tf_op jit(solution)/shard_map/all_gather | solution.py:209
  115.4 0.8 copy.6
  (2 shorter events, 0.1 us)
Async XLA Ops:
  3.6 17.9 %collective-permute-start.1 = (bf16[2,48,1664]{2,1,0:T(8,128)(2,1)}, bf16[2,48,1664]{2,1,0:T(8,128)(2,1)S(1)}, u32[]{:S(2)}, u32[]{:S(2)}) collective-permute-start(bf16[2,48,1664]{2,1,0:T(8,128)(2,1)} %get-tuple-element.19), channel_id=1, source_target_pairs={{0,64},{64,128},{128,192},{192,256},{256,320},{320,384},{384,448},... | collective-permute-start | bytes 958472 | tf_op jit(solution)/shard_map/ppermute | solution.py:105
  7.7 13.8 %collective-permute-start.2 = (bf16[2,48,1664]{2,1,0:T(8,128)(2,1)}, bf16[2,48,1664]{2,1,0:T(8,128)(2,1)S(1)}, u32[]{:S(2)}, u32[]{:S(2)}) collective-permute-start(bf16[2,48,1664]{2,1,0:T(8,128)(2,1)} %get-tuple-element.20), channel_id=1, source_target_pairs={{0,448},{64,0},{128,64},{192,128},{256,192},{320,256},{384,320},{4... | collective-permute-start | bytes 958472 | tf_op jit(solution)/shard_map/ppermute | solution.py:105
  11.5 10.0 %collective-permute-start = (bf16[48,1664]{1,0:T(8,128)(2,1)}, bf16[48,1664]{1,0:T(8,128)(2,1)S(1)}, u32[]{:S(2)}, u32[]{:S(2)}) collective-permute-start(bf16[48,1664]{1,0:T(8,128)(2,1)} %get-tuple-element.18), channel_id=1, source_target_pairs={{0,384},{1,129},{64,448},{65,193},{128,0},{129,257},{192,64},{193,... | collective-permute-start | bytes 479240 | tf_op jit(solution)/shard_map/ppermute | solution.py:113
  21.5 1.2 %copy-start = (f32[3,48,1664]{2,1,0:T(8,128)S(1)}, f32[3,48,1664]{2,1,0:T(8,128)}, u32[]{:S(2)}) copy-start(f32[3,48,1664]{2,1,0:T(8,128)} %shard_map.47.keep) | copy-start | bytes 2875396
  22.9 8.7 %collective-permute-start.3 = (bf16[48,1664]{1,0:T(8,128)(2,1)S(1)}, bf16[48,1664]{1,0:T(8,128)(2,1)S(1)}, u32[]{:S(2)}, u32[]{:S(2)}) collective-permute-start(bf16[48,1664]{1,0:T(8,128)(2,1)S(1)} %get-tuple-element.22), channel_id=1, source_target_pairs={{0,384},{64,448},{128,0},{192,64},{256,128},{320,192},{384,256},{4... | collective-permute-start | bytes 479240 | tf_op jit(solution)/shard_map/ppermute | solution.py:105
  26.4 8.2 %collective-permute-start.4 = (bf16[48,1664]{1,0:T(8,128)(2,1)S(1)}, bf16[48,1664]{1,0:T(8,128)(2,1)S(1)}, u32[]{:S(2)}, u32[]{:S(2)}) collective-permute-start(bf16[48,1664]{1,0:T(8,128)(2,1)S(1)} %get-tuple-element.23), channel_id=1, source_target_pairs={{0,128},{64,192},{128,256},{192,320},{256,384},{320,448},{384,0},{... | collective-permute-start | bytes 479240 | tf_op jit(solution)/shard_map/ppermute | solution.py:105
  48.3 19.6 %copy-start.1 = (bf16[832,768]{1,0:T(8,128)(2,1)S(1)}, bf16[832,768]{1,0:T(8,128)(2,1)}, u32[]{:S(2)}) copy-start(bf16[832,768]{1,0:T(8,128)(2,1)} %weight.1) | copy-start | bytes 3833860

commit v7 on v6

--- a/solution.py
+++ b/solution.py
@@ -46,11 +46,12 @@
         downs[at] = sent[(3 + at) * chunk : (4 + at) * chunk]
 
 
-def keep_kernel(place, tokens, gate, up, keep, *scratch):
+def keep_kernel(place, tokens, gate, up, keep, own, *scratch):
     chunk = keep.shape[1]
     out = blocks_of(KEPT, place, tokens, gate, up, *scratch)
-    for at in range(3):
-        keep[at] = out[at * chunk : (at + 1) * chunk]
+    own[...] = out[:chunk]
+    for at in range(2):
+        keep[at] = out[(at + 1) * chunk : (at + 2) * chunk]
 
 
 def front(flat, gate_weight, up_weight):
@@ -85,8 +86,9 @@
     one = jax.ShapeDtypeStruct((chunk, units), jnp.bfloat16)
     two = jax.ShapeDtypeStruct((2, chunk, units), jnp.bfloat16)
     far, ups, downs = call(send_kernel, SENT, [one, two, two])
-    (keep,) = call(keep_kernel, KEPT, [jax.ShapeDtypeStruct((3, chunk, units), jnp.float32)])
-    return far, ups, downs, keep
+    kept = jax.ShapeDtypeStruct((2, chunk, units), jnp.float32)
+    keep, own = call(keep_kernel, KEPT, [kept, jax.ShapeDtypeStruct((chunk, units), jnp.float32)])
+    return far, ups, downs, keep, own
 
 
 def exchange(blocks, axes):
@@ -130,18 +132,18 @@
     )(*operands)
 
 
-def merge_kernel(core, far, up, down, keep, down_two, up_two, base):
+def merge_kernel(core, far, up, down, keep, down_two, up_two):
     wide = jnp.float32
     to_up = jnp.where(core[0] == 0, 0.0, 1.0).astype(wide)
     far_rows = far[...].astype(wide)
-    up_two[...] = (keep[1] + up[1].astype(wide) + far_rows * to_up).astype(jnp.bfloat16)
-    down_two[...] = (keep[2] + down[1].astype(wide) + far_rows * (1.0 - to_up)).astype(jnp.bfloat16)
-    base[...] = keep[0] + up[0].astype(wide) + down[0].astype(wide)
-
-
-def finish_kernel(base, last_up, last_down, near, rest):
+    up_two[...] = (keep[0] + up[1].astype(wide) + far_rows * to_up).astype(jnp.bfloat16)
+    down_two[...] = (keep[1] + down[1].astype(wide) + far_rows * (1.0 - to_up)).astype(jnp.bfloat16)
+
+
+def finish_kernel(own, up, down, last_up, last_down, near, rest):
     wide = jnp.float32
-    y_sum = base[...] + last_up[...].astype(wide) + last_down[...].astype(wide)
+    y_sum = own[...] + up[0].astype(wide) + down[0].astype(wide)
+    y_sum = y_sum + last_up[...].astype(wide) + last_down[...].astype(wide)
     rounded = y_sum.astype(jnp.bfloat16)
     near[...] = rounded
     rest[...] = y_sum - rounded.astype(wide)
@@ -167,20 +169,20 @@
     give[...] = jnp.dot(left, weight[:, other], preferred_element_type=jnp.float32).astype(jnp.bfloat16)
 
 
-def scatter_sum(far, ups, downs, keep):
+def scatter_sum(far, ups, downs, keep, own):
     core = lax.axis_index("c").astype(jnp.int32).reshape(1)
     far = shift_by_core(far, -2)
     up = shift(ups, 1)
     down = shift(downs, -1)
     one = far.shape
-    down_two, up_two, base = small_call(
+    down_two, up_two = small_call(
         merge_kernel,
-        ((one, jnp.bfloat16), (one, jnp.bfloat16), (one, jnp.float32)),
+        ((one, jnp.bfloat16), (one, jnp.bfloat16)),
         core, far, up, down, keep, smem=1,
     )
     last_down = shift(down_two, -2)
     last_up = shift(up_two, 2)
-    return small_call(finish_kernel, ((one, jnp.bfloat16), (one, jnp.float32)), base, last_down, last_up)
+    return small_call(finish_kernel, ((one, jnp.bfloat16), (one, jnp.float32)), own, up, down, last_down, last_up)
 
 
 def body(tokens, gate_weight, up_weight, down_weight):

time: 117 us -> 117 us (level)
  no operation moved by 1% of the time
where the time goes in v7:
time: 117 us; the launch traced here: 116 us
  blocking collectives  79.3 us (68%)
  starting transfers between devices  16.5 us (14%)
  waiting for transfers between devices  9.46 us (8%)
  Pallas kernels  8.62 us (7%)
  local copies, waits for them, and re-layouts  1.93 us (2%)
    all_to_all x3, blocking collectives, exchange(): return lax.all_to_all(blocks, axes, 0, 0, tiled=True)  51.8 us
    ppermute x4, starting transfers between devices, shift(): return lax.ppermute(block, 'y', [(i, (i + step) % 8) for i in range(8)])  14 us
    all_gather x1, blocking collectives, body(): halves = lax.all_gather(near, 'zh', axis=0, tiled=True)  13.6 us
    all_gather x1, blocking collectives, body(): given = lax.all_gather(give, 'c', axis=0)  10.1 us
    pallas_call x2, Pallas kernels, call(): pl.pallas_call(kernel, out_shape=out_shapes, in_specs=[pl.BlockSpec(memor...  7.28 us
    ppermute x4, waiting for transfers between devices, shift(): return lax.ppermute(block, 'y', [(i, (i + step) % 8) for i in range(8)])  5.59 us
    ppermute x1, waiting for transfers between devices, shift_by_core(): return lax.ppermute(block, ('y', 'c'), pairs)  3.87 us
    all_gather x1, blocking collectives, body(): out = lax.all_gather(out_half, 'c', axis=1, tiled=True)  3.81 us
  transfers between devices with their start and end apart: 5, of which 3 were waited for; matrix products, arithmetic and copies ran while one was open for 0% of the time, Pallas kernels for 3%

profile of v7, /device:TPU:1, one launch (start us, length us, event | category | flops | bytes accessed | tf_op | source)
XLA Modules:
  0.0 116.1 jit_solution(13018708551421681715)
XLA Ops:
  0.0 3.6 %shard_map.47 = (bf16[48,1664]{1,0:T(8,128)(2,1)}, bf16[2,48,1664]{2,1,0:T(8,128)(2,1)}, bf16[2,48,1664]{2,1,0:T(8,128)(2,1)}) custom-call(s32[1]{0:T(128)} %bitcast.place, bf16[384,768]{1,0:T(8,128)(2,1)} %bitcast.8, bf16[832,768]{1,0:T(8,128)(2,1)} %gate.3, bf16[832,768]{1,0:T(8,128)(2,1)} %up.3), custom_call_target="tpu_custom_call" | custom-call | flops 613416960 | bytes 2924544 | tf_op jit(solution)/shard_map/pallas_call | solution.py:67
  3.6 4.0 %collective-permute-start = (bf16[2,48,1664]{2,1,0:T(8,128)(2,1)}, bf16[2,48,1664]{2,1,0:T(8,128)(2,1)S(1)}, u32[]{:S(2)}, u32[]{:S(2)}) collective-permute-start(bf16[2,48,1664]{2,1,0:T(8,128)(2,1)} %get-tuple-element.20), channel_id=1, source_target_pairs={{0,64},{64,128},{128,192},{192,256},{256,320},{320,384},{384,448},... | collective-permute-start | bytes 958472 | tf_op jit(solution)/shard_map/ppermute | solution.py:107
  7.7 3.8 %collective-permute-start.1 = (bf16[2,48,1664]{2,1,0:T(8,128)(2,1)}, bf16[2,48,1664]{2,1,0:T(8,128)(2,1)S(1)}, u32[]{:S(2)}, u32[]{:S(2)}) collective-permute-start(bf16[2,48,1664]{2,1,0:T(8,128)(2,1)} %get-tuple-element.21), channel_id=1, source_target_pairs={{0,448},{64,0},{128,64},{192,128},{256,192},{320,256},{384,320},{4... | collective-permute-start | bytes 958472 | tf_op jit(solution)/shard_map/ppermute | solution.py:107
  11.5 2.5 %collective-permute-start.2 = (bf16[48,1664]{1,0:T(8,128)(2,1)}, bf16[48,1664]{1,0:T(8,128)(2,1)S(1)}, u32[]{:S(2)}, u32[]{:S(2)}) collective-permute-start(bf16[48,1664]{1,0:T(8,128)(2,1)} %get-tuple-element.22), channel_id=1, source_target_pairs={{0,384},{1,129},{64,448},{65,193},{128,0},{129,257},{192,64},{193,... | collective-permute-start | bytes 479240 | tf_op jit(solution)/shard_map/ppermute | solution.py:115
  14.0 3.6 %shard_map.46 = (f32[2,48,1664]{2,1,0:T(8,128)}, f32[48,1664]{1,0:T(8,128)}) custom-call(s32[1]{0:T(128)} %bitcast.place, bf16[384,768]{1,0:T(8,128)(2,1)} %bitcast.9, bf16[832,768]{1,0:T(8,128)(2,1)} %gate.3, bf16[832,768]{1,0:T(8,128)(2,1)} %up.3), custom_call_target="tpu_custom_call" | custom-call | flops 368050176 | bytes 2777088 | tf_op jit(solution)/shard_map/pallas_call | solution.py:67
  17.6 3.9 %collective-permute-done.2.far = bf16[48,1664]{1,0:T(8,128)(2,1)S(1)} collective-permute-done((bf16[48,1664]{1,0:T(8,128)(2,1)}, bf16[48,1664]{1,0:T(8,128)(2,1)S(1)}, u32[]{:S(2)}, u32[]{:S(2)}) %collective-permute-start.2) | collective-permute-done | bytes 159776 | tf_op jit(solution)/shard_map/ppermute | solution.py:115
  21.5 0.0 collective-permute-done.up
  21.5 0.0 collective-permute-done.1.down
  21.5 0.0 copy-start.1
  21.5 1.1 copy-done.1
  22.6 0.0 copy-start.2
  22.6 0.1 shard_map.48
  22.7 3.6 %collective-permute-start.3 = (bf16[48,1664]{1,0:T(8,128)(2,1)S(1)}, bf16[48,1664]{1,0:T(8,128)(2,1)S(1)}, u32[]{:S(2)}, u32[]{:S(2)}) collective-permute-start(bf16[48,1664]{1,0:T(8,128)(2,1)S(1)} %get-tuple-element.24), channel_id=1, source_target_pairs={{0,384},{64,448},{128,0},{192,64},{256,128},{320,192},{384,256},{4... | collective-permute-start | bytes 479240 | tf_op jit(solution)/shard_map/ppermute | solution.py:107
  26.3 2.6 %collective-permute-start.4 = (bf16[48,1664]{1,0:T(8,128)(2,1)S(1)}, bf16[48,1664]{1,0:T(8,128)(2,1)S(1)}, u32[]{:S(2)}, u32[]{:S(2)}) collective-permute-start(bf16[48,1664]{1,0:T(8,128)(2,1)S(1)} %get-tuple-element.25), channel_id=1, source_target_pairs={{0,128},{64,192},{128,256},{192,320},{256,384},{320,448},{384,0},{... | collective-permute-start | bytes 479240 | tf_op jit(solution)/shard_map/ppermute | solution.py:107
  28.9 2.5 %collective-permute-done.3.last_up = bf16[48,1664]{1,0:T(8,128)(2,1)S(1)} collective-permute-done((bf16[48,1664]{1,0:T(8,128)(2,1)S(1)}, bf16[48,1664]{1,0:T(8,128)(2,1)S(1)}, u32[]{:S(2)}, u32[]{:S(2)}) %collective-permute-start.3) | collective-permute-done | bytes 159776 | tf_op jit(solution)/shard_map/ppermute | solution.py:107
  31.4 3.1 %collective-permute-done.4.last_down = bf16[48,1664]{1,0:T(8,128)(2,1)S(1)} collective-permute-done((bf16[48,1664]{1,0:T(8,128)(2,1)S(1)}, bf16[48,1664]{1,0:T(8,128)(2,1)S(1)}, u32[]{:S(2)}, u32[]{:S(2)}) %collective-permute-start.4) | collective-permute-done | bytes 159776 | tf_op jit(solution)/shard_map/ppermute | solution.py:107
  34.5 0.0 copy-done.2
  34.5 0.1 shard_map.49
  34.7 13.6 %all_gather.12.halves = bf16[96,1664]{1,0:T(8,128)(2,1)S(1)} all-gather(bf16[48,1664]{1,0:T(8,128)(2,1)S(1)} %get-tuple-element.26), channel_id=1, replica_groups=mesh['y'=8,'zh'=2,'zl'=4,'x'=4,'c'=2] {'zh'}, dimensions={0}, use_global_device_ids=true | all-gather | bytes 479232 | tf_op jit(solution)/shard_map/all_gather | solution.py:194
  48.3 0.0 copy-start
  48.3 0.1 shard_map.50
  48.4 19.5 %all_to_all.15.hidden = bf16[8,48,832]{2,1,0:T(8,128)(2,1)S(1)} all-to-all(bf16[8,48,832]{2,1,0:T(8,128)(2,1)S(1)} %shard_map.50), channel_id=1, replica_groups=mesh['y'=8,'zh'=2,'zl'=4,'x'=4,'c'=2] {'y'}, dimensions={0} | all-to-all | bytes 1277952 | tf_op jit(solution)/shard_map/all_to_all | solution.py:95
  67.9 0.0 copy-done
  67.9 0.9 shard_map.51
  68.8 10.1 %all-gather = bf16[768,384]{1,0:T(8,128)(2,1)S(1)} all-gather(bf16[384,384]{1,0:T(8,128)(2,1)S(1)} %get-tuple-element.32), channel_id=2, replica_groups=mesh['y'=8,'zh'=2,'zl'=4,'x'=4,'c'=2] {'c'}, dimensions={0}, use_global_device_ids=true | all-gather | bytes 884736 | tf_op jit(solution)/shard_map/all_gather | solution.py:206
  78.9 0.1 fusion
  79.0 18.1 %all_to_all.16 = bf16[16,24,384]{2,1,0:T(8,128)(2,1)S(1)} all-to-all(bf16[16,24,384]{2,1,0:T(8,128)(2,1)S(1)} %bitcast.11), channel_id=1, replica_groups=mesh['y'=8,'zh'=2,'zl'=4,'x'=4,'c'=2] {'x','zl'}, dimensions={0} | all-to-all | bytes 589824 | tf_op jit(solution)/shard_map/all_to_all | solution.py:95
  97.2 14.2 %all_to_all.17 = bf16[16,24,384]{2,1,0:T(8,128)(2,1)S(1)} all-to-all(bf16[16,24,384]{2,1,0:T(8,128)(2,1)S(1)} %broadcast_in_dim.2), channel_id=1, replica_groups=mesh['y'=8,'zh'=2,'zl'=4,'x'=4,'c'=2] {'x','zl'}, dimensions={0} | all-to-all | bytes 589824 | tf_op jit(solution)/shard_map/all_to_all | solution.py:95
  111.5 3.8 %all_gather.15 = bf16[384,768]{1,0:T(8,128)(2,1)S(1)} all-gather(bf16[384,384]{1,0:T(8,128)(2,1)S(1)} %bitcast.10), channel_id=1, replica_groups=mesh['y'=8,'zh'=2,'zl'=4,'x'=4,'c'=2] {'c'}, dimensions={1}, use_global_device_ids=true | all-gather | bytes 884736 | tf_op jit(solution)/shard_map/all_gather | solution.py:211
  115.3 0.8 copy.6
  (2 shorter events, 0.1 us)
Async XLA Ops:
  3.6 17.9 %collective-permute-start = (bf16[2,48,1664]{2,1,0:T(8,128)(2,1)}, bf16[2,48,1664]{2,1,0:T(8,128)(2,1)S(1)}, u32[]{:S(2)}, u32[]{:S(2)}) collective-permute-start(bf16[2,48,1664]{2,1,0:T(8,128)(2,1)} %get-tuple-element.20), channel_id=1, source_target_pairs={{0,64},{64,128},{128,192},{192,256},{256,320},{320,384},{384,448},... | collective-permute-start | bytes 958472 | tf_op jit(solution)/shard_map/ppermute | solution.py:107
  7.7 13.8 %collective-permute-start.1 = (bf16[2,48,1664]{2,1,0:T(8,128)(2,1)}, bf16[2,48,1664]{2,1,0:T(8,128)(2,1)S(1)}, u32[]{:S(2)}, u32[]{:S(2)}) collective-permute-start(bf16[2,48,1664]{2,1,0:T(8,128)(2,1)} %get-tuple-element.21), channel_id=1, source_target_pairs={{0,448},{64,0},{128,64},{192,128},{256,192},{320,256},{384,320},{4... | collective-permute-start | bytes 958472 | tf_op jit(solution)/shard_map/ppermute | solution.py:107
  11.5 10.0 %collective-permute-start.2 = (bf16[48,1664]{1,0:T(8,128)(2,1)}, bf16[48,1664]{1,0:T(8,128)(2,1)S(1)}, u32[]{:S(2)}, u32[]{:S(2)}) collective-permute-start(bf16[48,1664]{1,0:T(8,128)(2,1)} %get-tuple-element.22), channel_id=1, source_target_pairs={{0,384},{1,129},{64,448},{65,193},{128,0},{129,257},{192,64},{193,... | collective-permute-start | bytes 479240 | tf_op jit(solution)/shard_map/ppermute | solution.py:115
  21.5 1.1 copy-start.1
  22.6 11.9 %copy-start.2 = (f32[48,1664]{1,0:T(8,128)S(1)}, f32[48,1664]{1,0:T(8,128)}, u32[]{:S(2)}) copy-start(f32[48,1664]{1,0:T(8,128)} %get-tuple-element.19.own) | copy-start | bytes 958468
  22.7 8.7 %collective-permute-start.3 = (bf16[48,1664]{1,0:T(8,128)(2,1)S(1)}, bf16[48,1664]{1,0:T(8,128)(2,1)S(1)}, u32[]{:S(2)}, u32[]{:S(2)}) collective-permute-start(bf16[48,1664]{1,0:T(8,128)(2,1)S(1)} %get-tuple-element.24), channel_id=1, source_target_pairs={{0,384},{64,448},{128,0},{192,64},{256,128},{320,192},{384,256},{4... | collective-permute-start | bytes 479240 | tf_op jit(solution)/shard_map/ppermute | solution.py:107
  26.3 8.2 %collective-permute-start.4 = (bf16[48,1664]{1,0:T(8,128)(2,1)S(1)}, bf16[48,1664]{1,0:T(8,128)(2,1)S(1)}, u32[]{:S(2)}, u32[]{:S(2)}) collective-permute-start(bf16[48,1664]{1,0:T(8,128)(2,1)S(1)} %get-tuple-element.25), channel_id=1, source_target_pairs={{0,128},{64,192},{128,256},{192,320},{256,384},{320,448},{384,0},{... | collective-permute-start | bytes 479240 | tf_op jit(solution)/shard_map/ppermute | solution.py:107
  48.3 19.6 %copy-start = (bf16[832,768]{1,0:T(8,128)(2,1)S(1)}, bf16[832,768]{1,0:T(8,128)(2,1)}, u32[]{:S(2)}) copy-start(bf16[832,768]{1,0:T(8,128)(2,1)} %weight.1) | copy-start | bytes 3833860

commit v8 on v7

--- a/solution.py
+++ b/solution.py
@@ -208,8 +208,7 @@
     chip = chip.astype(jnp.bfloat16).reshape(16, rows // 16, half)
     out_share = total(exchange(chip, PLANE)).astype(jnp.bfloat16)
     out_half = spread(out_share, PLANE, 16).reshape(rows, half)
-    out = lax.all_gather(out_half, "c", axis=1, tiled=True)
-    return out.reshape(steps, batch, width)
+    return lax.all_gather(out_half.reshape(steps, batch, half), "c", axis=2, tiled=True)
 
 
 def solution(mesh):

time: 117 us -> 117 us (level)
  no operation moved by 1% of the time
where the time goes in v8:
time: 117 us; the launch traced here: 116 us
  blocking collectives  79.3 us (68%)
  starting transfers between devices  16.5 us (14%)
  waiting for transfers between devices  9.46 us (8%)
  Pallas kernels  8.62 us (7%)
  local copies, waits for them, and re-layouts  1.93 us (2%)
    all_to_all x3, blocking collectives, exchange(): return lax.all_to_all(blocks, axes, 0, 0, tiled=True)  51.8 us
    ppermute x4, starting transfers between devices, shift(): return lax.ppermute(block, 'y', [(i, (i + step) % 8) for i in range(8)])  14 us
    all_gather x1, blocking collectives, body(): halves = lax.all_gather(near, 'zh', axis=0, tiled=True)  13.6 us
    all_gather x1, blocking collectives, body(): given = lax.all_gather(give, 'c', axis=0)  10.1 us
    pallas_call x2, Pallas kernels, call(): pl.pallas_call(kernel, out_shape=out_shapes, in_specs=[pl.BlockSpec(memor...  7.28 us
    ppermute x4, waiting for transfers between devices, shift(): return lax.ppermute(block, 'y', [(i, (i + step) % 8) for i in range(8)])  5.59 us
    ppermute x1, waiting for transfers between devices, shift_by_core(): return lax.ppermute(block, ('y', 'c'), pairs)  3.87 us
    all_gather x1, blocking collectives, body(): lax.all_gather(out_half.reshape(steps, batch, half), 'c', axis=2, tiled=T...  3.81 us
  transfers between devices with their start and end apart: 5, of which 3 were waited for; matrix products, arithmetic and copies ran while one was open for 0% of the time, Pallas kernels for 3%

profile of v8, /device:TPU:1, one launch (start us, length us, event | category | flops | bytes accessed | tf_op | source)
XLA Modules:
  0.0 116.1 jit_solution(13018708551421681715)
XLA Ops:
  0.0 3.6 %shard_map.47 = (bf16[48,1664]{1,0:T(8,128)(2,1)}, bf16[2,48,1664]{2,1,0:T(8,128)(2,1)}, bf16[2,48,1664]{2,1,0:T(8,128)(2,1)}) custom-call(s32[1]{0:T(128)} %bitcast.place, bf16[384,768]{1,0:T(8,128)(2,1)} %bitcast.6, bf16[832,768]{1,0:T(8,128)(2,1)} %gate.3, bf16[832,768]{1,0:T(8,128)(2,1)} %up.3), custom_call_target="tpu_custom_call" | custom-call | flops 613416960 | bytes 2924544 | tf_op jit(solution)/shard_map/pallas_call | solution.py:67
  3.6 4.0 %collective-permute-start = (bf16[2,48,1664]{2,1,0:T(8,128)(2,1)}, bf16[2,48,1664]{2,1,0:T(8,128)(2,1)S(1)}, u32[]{:S(2)}, u32[]{:S(2)}) collective-permute-start(bf16[2,48,1664]{2,1,0:T(8,128)(2,1)} %get-tuple-element.20), channel_id=1, source_target_pairs={{0,64},{64,128},{128,192},{192,256},{256,320},{320,384},{384,448},... | collective-permute-start | bytes 958472 | tf_op jit(solution)/shard_map/ppermute | solution.py:107
  7.7 3.8 %collective-permute-start.1 = (bf16[2,48,1664]{2,1,0:T(8,128)(2,1)}, bf16[2,48,1664]{2,1,0:T(8,128)(2,1)S(1)}, u32[]{:S(2)}, u32[]{:S(2)}) collective-permute-start(bf16[2,48,1664]{2,1,0:T(8,128)(2,1)} %get-tuple-element.21), channel_id=1, source_target_pairs={{0,448},{64,0},{128,64},{192,128},{256,192},{320,256},{384,320},{4... | collective-permute-start | bytes 958472 | tf_op jit(solution)/shard_map/ppermute | solution.py:107
  11.5 2.5 %collective-permute-start.2 = (bf16[48,1664]{1,0:T(8,128)(2,1)}, bf16[48,1664]{1,0:T(8,128)(2,1)S(1)}, u32[]{:S(2)}, u32[]{:S(2)}) collective-permute-start(bf16[48,1664]{1,0:T(8,128)(2,1)} %get-tuple-element.22), channel_id=1, source_target_pairs={{0,384},{1,129},{64,448},{65,193},{128,0},{129,257},{192,64},{193,... | collective-permute-start | bytes 479240 | tf_op jit(solution)/shard_map/ppermute | solution.py:115
  14.0 3.6 %shard_map.46 = (f32[2,48,1664]{2,1,0:T(8,128)}, f32[48,1664]{1,0:T(8,128)}) custom-call(s32[1]{0:T(128)} %bitcast.place, bf16[384,768]{1,0:T(8,128)(2,1)} %bitcast.7, bf16[832,768]{1,0:T(8,128)(2,1)} %gate.3, bf16[832,768]{1,0:T(8,128)(2,1)} %up.3), custom_call_target="tpu_custom_call" | custom-call | flops 368050176 | bytes 2777088 | tf_op jit(solution)/shard_map/pallas_call | solution.py:67
  17.6 3.9 %collective-permute-done.2.far = bf16[48,1664]{1,0:T(8,128)(2,1)S(1)} collective-permute-done((bf16[48,1664]{1,0:T(8,128)(2,1)}, bf16[48,1664]{1,0:T(8,128)(2,1)S(1)}, u32[]{:S(2)}, u32[]{:S(2)}) %collective-permute-start.2) | collective-permute-done | bytes 159776 | tf_op jit(solution)/shard_map/ppermute | solution.py:115
  21.5 0.0 collective-permute-done.up
  21.5 0.0 collective-permute-done.1.down
  21.5 0.0 copy-start.1
  21.5 1.1 copy-done.1
  22.6 0.0 copy-start.2
  22.6 0.1 shard_map.48
  22.7 3.6 %collective-permute-start.3 = (bf16[48,1664]{1,0:T(8,128)(2,1)S(1)}, bf16[48,1664]{1,0:T(8,128)(2,1)S(1)}, u32[]{:S(2)}, u32[]{:S(2)}) collective-permute-start(bf16[48,1664]{1,0:T(8,128)(2,1)S(1)} %get-tuple-element.24), channel_id=1, source_target_pairs={{0,384},{64,448},{128,0},{192,64},{256,128},{320,192},{384,256},{4... | collective-permute-start | bytes 479240 | tf_op jit(solution)/shard_map/ppermute | solution.py:107
  26.3 2.6 %collective-permute-start.4 = (bf16[48,1664]{1,0:T(8,128)(2,1)S(1)}, bf16[48,1664]{1,0:T(8,128)(2,1)S(1)}, u32[]{:S(2)}, u32[]{:S(2)}) collective-permute-start(bf16[48,1664]{1,0:T(8,128)(2,1)S(1)} %get-tuple-element.25), channel_id=1, source_target_pairs={{0,128},{64,192},{128,256},{192,320},{256,384},{320,448},{384,0},{... | collective-permute-start | bytes 479240 | tf_op jit(solution)/shard_map/ppermute | solution.py:107
  28.9 2.5 %collective-permute-done.3.last_up = bf16[48,1664]{1,0:T(8,128)(2,1)S(1)} collective-permute-done((bf16[48,1664]{1,0:T(8,128)(2,1)S(1)}, bf16[48,1664]{1,0:T(8,128)(2,1)S(1)}, u32[]{:S(2)}, u32[]{:S(2)}) %collective-permute-start.3) | collective-permute-done | bytes 159776 | tf_op jit(solution)/shard_map/ppermute | solution.py:107
  31.4 3.1 %collective-permute-done.4.last_down = bf16[48,1664]{1,0:T(8,128)(2,1)S(1)} collective-permute-done((bf16[48,1664]{1,0:T(8,128)(2,1)S(1)}, bf16[48,1664]{1,0:T(8,128)(2,1)S(1)}, u32[]{:S(2)}, u32[]{:S(2)}) %collective-permute-start.4) | collective-permute-done | bytes 159776 | tf_op jit(solution)/shard_map/ppermute | solution.py:107
  34.5 0.0 copy-done.2
  34.5 0.1 shard_map.49
  34.7 13.6 %all_gather.12.halves = bf16[96,1664]{1,0:T(8,128)(2,1)S(1)} all-gather(bf16[48,1664]{1,0:T(8,128)(2,1)S(1)} %get-tuple-element.26), channel_id=1, replica_groups=mesh['y'=8,'zh'=2,'zl'=4,'x'=4,'c'=2] {'zh'}, dimensions={0}, use_global_device_ids=true | all-gather | bytes 479232 | tf_op jit(solution)/shard_map/all_gather | solution.py:194
  48.3 0.0 copy-start
  48.3 0.1 shard_map.50
  48.4 19.5 %all_to_all.15.hidden = bf16[8,48,832]{2,1,0:T(8,128)(2,1)S(1)} all-to-all(bf16[8,48,832]{2,1,0:T(8,128)(2,1)S(1)} %shard_map.50), channel_id=1, replica_groups=mesh['y'=8,'zh'=2,'zl'=4,'x'=4,'c'=2] {'y'}, dimensions={0} | all-to-all | bytes 1277952 | tf_op jit(solution)/shard_map/all_to_all | solution.py:95
  67.9 0.0 copy-done
  67.9 0.9 shard_map.51
  68.8 10.1 %all-gather = bf16[768,384]{1,0:T(8,128)(2,1)S(1)} all-gather(bf16[384,384]{1,0:T(8,128)(2,1)S(1)} %get-tuple-element.32), channel_id=2, replica_groups=mesh['y'=8,'zh'=2,'zl'=4,'x'=4,'c'=2] {'c'}, dimensions={0}, use_global_device_ids=true | all-gather | bytes 884736 | tf_op jit(solution)/shard_map/all_gather | solution.py:206
  78.9 0.1 fusion
  79.0 18.1 %all_to_all.16 = bf16[16,24,384]{2,1,0:T(8,128)(2,1)S(1)} all-to-all(bf16[16,24,384]{2,1,0:T(8,128)(2,1)S(1)} %bitcast.9), channel_id=1, replica_groups=mesh['y'=8,'zh'=2,'zl'=4,'x'=4,'c'=2] {'x','zl'}, dimensions={0} | all-to-all | bytes 589824 | tf_op jit(solution)/shard_map/all_to_all | solution.py:95
  97.2 14.2 %all_to_all.17 = bf16[16,24,384]{2,1,0:T(8,128)(2,1)S(1)} all-to-all(bf16[16,24,384]{2,1,0:T(8,128)(2,1)S(1)} %broadcast_in_dim.2), channel_id=1, replica_groups=mesh['y'=8,'zh'=2,'zl'=4,'x'=4,'c'=2] {'x','zl'}, dimensions={0} | all-to-all | bytes 589824 | tf_op jit(solution)/shard_map/all_to_all | solution.py:95
  111.5 3.8 %all_gather.15 = bf16[2,192,768]{2,1,0:T(8,128)(2,1)S(1)} all-gather(bf16[2,192,384]{2,1,0:T(8,128)(2,1)S(1)} %bitcast.8), channel_id=1, replica_groups=mesh['y'=8,'zh'=2,'zl'=4,'x'=4,'c'=2] {'c'}, dimensions={2}, use_global_device_ids=true | all-gather | bytes 884736 | tf_op jit(solution)/shard_map/all_gather | solution.py:211
  115.3 0.8 copy.6
  (2 shorter events, 0.1 us)
Async XLA Ops:
  3.6 17.9 %collective-permute-start = (bf16[2,48,1664]{2,1,0:T(8,128)(2,1)}, bf16[2,48,1664]{2,1,0:T(8,128)(2,1)S(1)}, u32[]{:S(2)}, u32[]{:S(2)}) collective-permute-start(bf16[2,48,1664]{2,1,0:T(8,128)(2,1)} %get-tuple-element.20), channel_id=1, source_target_pairs={{0,64},{64,128},{128,192},{192,256},{256,320},{320,384},{384,448},... | collective-permute-start | bytes 958472 | tf_op jit(solution)/shard_map/ppermute | solution.py:107
  7.7 13.8 %collective-permute-start.1 = (bf16[2,48,1664]{2,1,0:T(8,128)(2,1)}, bf16[2,48,1664]{2,1,0:T(8,128)(2,1)S(1)}, u32[]{:S(2)}, u32[]{:S(2)}) collective-permute-start(bf16[2,48,1664]{2,1,0:T(8,128)(2,1)} %get-tuple-element.21), channel_id=1, source_target_pairs={{0,448},{64,0},{128,64},{192,128},{256,192},{320,256},{384,320},{4... | collective-permute-start | bytes 958472 | tf_op jit(solution)/shard_map/ppermute | solution.py:107
  11.5 10.0 %collective-permute-start.2 = (bf16[48,1664]{1,0:T(8,128)(2,1)}, bf16[48,1664]{1,0:T(8,128)(2,1)S(1)}, u32[]{:S(2)}, u32[]{:S(2)}) collective-permute-start(bf16[48,1664]{1,0:T(8,128)(2,1)} %get-tuple-element.22), channel_id=1, source_target_pairs={{0,384},{1,129},{64,448},{65,193},{128,0},{129,257},{192,64},{193,... | collective-permute-start | bytes 479240 | tf_op jit(solution)/shard_map/ppermute | solution.py:115
  21.5 1.1 copy-start.1
  22.6 11.9 %copy-start.2 = (f32[48,1664]{1,0:T(8,128)S(1)}, f32[48,1664]{1,0:T(8,128)}, u32[]{:S(2)}) copy-start(f32[48,1664]{1,0:T(8,128)} %get-tuple-element.19.own) | copy-start | bytes 958468
  22.7 8.7 %collective-permute-start.3 = (bf16[48,1664]{1,0:T(8,128)(2,1)S(1)}, bf16[48,1664]{1,0:T(8,128)(2,1)S(1)}, u32[]{:S(2)}, u32[]{:S(2)}) collective-permute-start(bf16[48,1664]{1,0:T(8,128)(2,1)S(1)} %get-tuple-element.24), channel_id=1, source_target_pairs={{0,384},{64,448},{128,0},{192,64},{256,128},{320,192},{384,256},{4... | collective-permute-start | bytes 479240 | tf_op jit(solution)/shard_map/ppermute | solution.py:107
  26.3 8.2 %collective-permute-start.4 = (bf16[48,1664]{1,0:T(8,128)(2,1)S(1)}, bf16[48,1664]{1,0:T(8,128)(2,1)S(1)}, u32[]{:S(2)}, u32[]{:S(2)}) collective-permute-start(bf16[48,1664]{1,0:T(8,128)(2,1)S(1)} %get-tuple-element.25), channel_id=1, source_target_pairs={{0,128},{64,192},{128,256},{192,320},{256,384},{320,448},{384,0},{... | collective-permute-start | bytes 479240 | tf_op jit(solution)/shard_map/ppermute | solution.py:107
  48.3 19.6 %copy-start = (bf16[832,768]{1,0:T(8,128)(2,1)S(1)}, bf16[832,768]{1,0:T(8,128)(2,1)}, u32[]{:S(2)}) copy-start(bf16[832,768]{1,0:T(8,128)(2,1)} %weight.1) | copy-start | bytes 3833860
